TPU v7x, 256 devices: a whole 4x4x8 slice. The times are simulated.
256 devices in a mesh: row: 4 (over x), col: 16 (over y_hi, z), seq: 4 (over y_lo, core).
Axes of the slice: x: 4, y: 4 (y_hi: 2, y_lo: 2; y = y_hi * 2 + y_lo), z: 8, core: 2. Of those that a mesh axis runs over, the one named last changes fastest.
Arguments:
- left: bfloat16 [128, 32, 768], P('seq', 'col', 'row'), may hold values from -6 to 6
- right: bfloat16 [128, 32, 768], P('seq', 'row', 'col'), may hold values from -6 to 6
- projection: bfloat16 [1024, 128], replicated, may hold values from -2 to 2
- bias: float32 [128], replicated, may hold values from -3 to 3
- cotangent: bfloat16 [768, 768, 128], P(('row', 'seq'), 'col'), may hold values from -1.1953125 to 1.1953125
Outputs:
- pair: bfloat16 [768, 768, 128], P(('row', 'seq'), 'col')
- left_grad: float32 [128, 32, 768], P('seq', 'col', 'row')
- right_grad: float32 [128, 32, 768], P('seq', 'row', 'col')
- weight_grad: float32 [1024, 128], replicated
All inputs are finite; a program needn't handle non-finite values.
Results may differ from a plain program's by a relative error of at most 0.019.
Values may be sent and summed in bfloat16 or wider, within the bound.
A program may use at most 128 MiB of HBM per device.

v0:
```python
import jax
import jax.numpy as jnp
from jax import lax
from jax.sharding import PartitionSpec as P

C = 32
CP = 128
S = 128


def pick_block(rows, largest):
    size = largest
    while rows % size != 0:
        size = size // 2
    return size


def body(left, right, projection, bias, cotangent):
    seq_local = left.shape[0]
    a_cols = lax.all_gather(left, "col", axis=1, tiled=True)
    b_rows = lax.all_gather(right, "row", axis=1, tiled=True)
    cols = b_rows.shape[2]
    w_t = projection.T
    dz_tile = lax.all_gather(cotangent, "seq", axis=0, tiled=True)
    rows = a_cols.shape[2]
    blk = pick_block(rows, 16)

    def step(carry, index):
        grad_w, grad_b = carry
        start = index * blk
        a_blk = lax.dynamic_slice_in_dim(a_cols, start, blk, 2)
        dz_flat = lax.dynamic_slice_in_dim(dz_tile, start, blk, 0).reshape(blk * cols, CP)
        outer = jnp.einsum("sci,sej->ijce", a_blk, b_rows, preferred_element_type=jnp.float32)
        outer = outer.reshape(blk * cols, C * C).astype(jnp.bfloat16)
        part = jnp.dot(outer, projection, preferred_element_type=jnp.float32).astype(jnp.bfloat16)
        grad_w = grad_w + jnp.dot(outer.T, dz_flat, preferred_element_type=jnp.float32)
        d_outer = (jnp.dot(dz_flat, w_t, preferred_element_type=jnp.float32) / S).astype(
            jnp.bfloat16
        )
        d_outer = d_outer.reshape(blk, cols, C, C)
        grad_a = jnp.einsum("ijce,sej->sci", d_outer, b_rows, preferred_element_type=jnp.float32)
        grad_b = grad_b + jnp.einsum(
            "ijce,sci->sej", d_outer, a_blk, preferred_element_type=jnp.float32
        )
        return ((grad_w, grad_b), (part, grad_a))

    init = (jnp.zeros((C * C, CP), jnp.float32), jnp.zeros((seq_local, C, cols), jnp.float32))
    (grad_w, grad_b), (parts, grads_a) = lax.scan(
        step, init, jnp.arange(rows // blk, dtype=jnp.int32)
    )
    parts = parts.reshape(rows, cols, CP).astype(jnp.float32)
    grads_a = jnp.transpose(grads_a, (1, 2, 0, 3)).reshape(seq_local, C, rows)
    summed = lax.psum_scatter(
        parts.astype(jnp.bfloat16), "seq", scatter_dimension=0, tiled=True
    ).astype(jnp.float32)
    pair = (summed / S + bias).astype(jnp.bfloat16)
    left_grad = lax.psum_scatter(
        grads_a.astype(jnp.bfloat16), "col", scatter_dimension=1, tiled=True
    ).astype(jnp.float32)
    right_grad = lax.psum_scatter(
        grad_b.astype(jnp.bfloat16), "row", scatter_dimension=1, tiled=True
    ).astype(jnp.float32)
    weight_grad = lax.psum(grad_w, ("row", "col", "seq")) / S
    return (pair, left_grad, right_grad, weight_grad)


def solution(mesh):
    placed = (
        P("seq", "col", "row"),
        P("seq", "row", "col"),
        P(),
        P(),
        P(("row", "seq"), "col", None),
    )
    return jax.shard_map(
        body,
        mesh=mesh,
        in_specs=placed,
        out_specs=(
            P(("row", "seq"), "col", None),
            P("seq", "col", "row"),
            P("seq", "row", "col"),
            P(),
        ),
        check_vma=False,
    )
```

profile of v0, /device:TPU:1, one launch (start us, length us, event | category | flops | bytes accessed | tf_op | source)
XLA Modules:
  0.0 1051.4 jit_solution(13298475947950371733)
XLA Ops:
  8.8 41.1 %all_gather.9 = bf16[32,32,192]{2,0,1:T(8,128)(2,1)S(1)} all-gather(bf16[32,2,192]{2,0,1:T(8,128)(2,1)S(1)} %copy.32), channel_id=1, replica_groups=mesh['row'=4,'col'=16,'seq'=4] {'col'}, dimensions={1}, use_global_device_ids=true | all-gather | bytes 417792 | tf_op jit(solution)/shard_map/all_gather | solution.py:20
  52.9 9.7 all_gather.10
  62.7 457.6 %while.17 = (s32[]{:T(128)}, f32[1024,128]{1,0:T(8,128)}, f32[32,32,48]{2,0,1:T(8,128)}, bf16[12,768,128]{2,1,0:T(8,128)(2,1)}, bf16[12,32,32,16]{1,3,2,0:T(8,12...) while((s32[]{:T(128)}, f32[1024,128]{1,0:T(8,128)}, ...), condition=%wide.region_1.2_spmd.clone, body=%wide.region_0.1_spmd.clone.sunk | while | flops 757792768 | bytes 38176140 | solution.py:48
  70.7 6.1 convert_element_type.75
  82.4 7.2 reshape.36
  107.9 6.1 convert_element_type.75
  120.6 7.2 reshape.36
  146.1 6.1 convert_element_type.75
  158.8 7.2 reshape.36
  184.3 6.1 convert_element_type.75
  197.0 7.2 reshape.36
  222.5 6.1 convert_element_type.75
  235.2 7.2 reshape.36
  260.7 6.1 convert_element_type.75
  273.4 7.2 reshape.36
  298.9 6.1 convert_element_type.75
  311.6 7.2 reshape.36
  337.1 6.1 convert_element_type.75
  349.8 7.2 reshape.36
  375.3 6.1 convert_element_type.75
  388.0 7.2 reshape.36
  395.2 4.9 fusion.53
  413.5 6.1 convert_element_type.75
  426.2 7.2 reshape.36
  451.7 6.1 convert_element_type.75
  464.4 7.2 reshape.36
  489.9 6.1 convert_element_type.75
  502.6 7.2 reshape.36
  529.9 17.4 %reduce-scatter.10.cloned.1.call-done = bf16[8,1536]{1,0:T(8,128)(2,1)} async-done(((bf16[32,1536]{1,0:T(8,128)(2,1)}), bf16[8,1536]{1,0:T(8,128)(2,1)}) %reduce-scatter.10.cloned.1.call-update) | async-done | bytes 24592
  548.9 257.9 %all-reduce.2.cloned.1.call-done = f32[1024,128]{1,0:T(8,128)} async-done(((f32[1024,128]{1,0:T(8,128)}), f32[1024,128]{1,0:T(8,128)}) %all-reduce.2.cloned.1.call-update) | async-done | bytes 524304 | tf_op jit(solution)/shard_map/psum | solution.py:63
  808.6 195.3 %reduce-scatter.8.cloned.1.call-done = bf16[32,2,192]{2,0,1:T(8,128)(2,1)} async-done(((bf16[32,32,192]{2,0,1:T(8,128)(2,1)}), bf16[32,2,192]{2,0,1:T(8,128)(2,1)}) %reduce-scatter.8.cloned.1.call-update) | async-done | bytes 24592 | tf_op jit(solution)/shard_map/reduce_scatter | solution.py:57
  1005.4 37.5 %reduce-scatter.6.cloned.1.call-done = bf16[48,48,128]{2,1,0:T(8,128)(2,1)} async-done(((bf16[192,48,128]{2,1,0:T(8,128)(2,1)}), bf16[48,48,128]{2,1,0:T(8,128)(2,1)}) %reduce-scatter.6.cloned.1.call-update) | async-done | bytes 589840 | tf_op jit(solution)/shard_map/reduce_scatter | solution.py:53
  (299 shorter events, 304.7 us)
Async XLA Ops:
  7.2 44.9 %copy-start.7 = (bf16[32,8,48]{2,1,0:T(8,128)(2,1)S(1)}, bf16[32,8,48]{2,1,0:T(8,128)(2,1)}, u32[]{:S(2)}) copy-start(bf16[32,8,48]{2,1,0:T(8,128)(2,1)} %param.8) | copy-start | bytes 73732
  7.2 55.5 %all-gather.2.cloned.1.call-start = ((), (), s32[]{:S(2)}) async-start(), calls=%async_computation.3 | async-start | bytes 2949120 | tf_op jit(solution)/shard_map/all_gather | solution.py:24
  7.9 44.2 %copy-start.5 = (bf16[1024,128]{1,0:T(8,128)(2,1)S(1)}, bf16[1024,128]{1,0:T(8,128)(2,1)}, u32[]{:S(2)}) copy-start(bf16[1024,128]{1,0:T(8,128)(2,1)} %param.9) | copy-start | bytes 786436
  7.9 539.4 %reduce-scatter.10.cloned.1.call-start = ((), (), s32[]{:S(2)}) async-start(), calls=%async_computation.7 | async-start | bytes 122880
  82.4 7.2 copy-start.3
  89.6 7.3 copy-start
  120.6 7.2 copy-start.3
  127.8 7.3 copy-start
  158.8 7.2 copy-start.3
  166.0 7.4 copy-start
  197.0 7.2 copy-start.3
  204.2 7.3 copy-start
  235.2 7.2 copy-start.3
  242.4 7.3 copy-start
  273.4 7.2 copy-start.3
  280.6 7.3 copy-start
  311.6 7.2 copy-start.3
  318.8 7.3 copy-start
  349.8 7.2 copy-start.3
  357.0 7.3 copy-start
  388.0 7.2 copy-start.3
  395.2 7.4 copy-start
  426.2 7.2 copy-start.3
  433.4 7.4 copy-start
  464.4 7.2 copy-start.3
  471.6 7.3 copy-start
  502.6 7.2 copy-start.3
  509.8 7.3 copy-start
  522.7 284.1 %all-reduce.2.cloned.1.call-start = ((), (), s32[]{:S(2)}) async-start(), calls=%async_computation.6 | async-start | bytes 1048576 | tf_op jit(solution)/shard_map/psum | solution.py:63
  523.4 480.5 %reduce-scatter.8.cloned.1.call-start = ((), (), s32[]{:S(2)}) async-start(), calls=%async_computation.5 | async-start | bytes 557056 | tf_op jit(solution)/shard_map/reduce_scatter | solution.py:57
  529.3 513.5 %reduce-scatter.6.cloned.1.call-start = ((), (), s32[]{:S(2)}) async-start(), calls=%async_computation.4 | async-start | bytes 2949120 | tf_op jit(solution)/shard_map/reduce_scatter | solution.py:53
  529.4 513.4 %copy-start.8 = (f32[128]{0:T(128)S(1)}, f32[128]{0:T(128)}, u32[]{:S(2)}) copy-start(f32[128]{0:T(128)} %param.10) | copy-start | bytes 1540
  (48 other events, 174.9 us)
Sparse Core Ops, SparseCore 0:
  9.8 41.5 all-gather.1
  522.8 24.4 reduce-scatter.9
  554.2 252.4 all-reduce.1
  811.5 192.4 reduce-scatter.7
  1006.3 36.4 reduce-scatter.5
where the time goes:
time: 1060 us; the launch traced here: 1050 us
  waiting for transfers between devices  510 us (48%)
  local copies, waits for them, and re-layouts  269 us (25%)
  matrix products  194 us (18%)
  blocking collectives  50.8 us (5%)
  between operations  13.9 us (1%)
    psum x1, waiting for transfers between devices, body(): weight_grad = lax.psum(grad_w, ('row', 'col', 'seq')) / S  258 us
    reduce_scatter x1, waiting for transfers between devices, body(): lax.psum_scatter(grads_a.astype(jnp.bfloat16), 'col', scatter_dimension=1...  195 us
    convert_element_type x24, local copies, waits for them, and re-layouts, step(): outer = outer.reshape(blk * cols, C * C).astype(jnp.bfloat16)  129 us
    reshape x12, local copies, waits for them, and re-layouts, step(): d_outer = d_outer.reshape(blk, cols, C, C)  86.5 us
    dot_general x12, matrix products, step(): jnp.einsum('ijce,sci->sej', d_outer, a_blk, preferred_element_type=jnp.fl...  58.4 us
    all_gather x1, blocking collectives, body(): a_cols = lax.all_gather(left, 'col', axis=1, tiled=True)  41.1 us
    reduce_scatter x1, waiting for transfers between devices, body(): lax.psum_scatter(parts.astype(jnp.bfloat16), 'seq', scatter_dimension=0,...  37.5 us
    dot_general x12, matrix products, step(): jnp.einsum('ijce,sej->sci', d_outer, b_rows, preferred_element_type=jnp.f...  34.8 us
  transfers between devices with their start and end apart: 5, of which 4 were waited for; matrix products, arithmetic and copies ran while one was open for 1% of the time, Pallas kernels for 0%

commit v1 on v0

v1 whole, which is shorter than its diff:
```python
import functools

import jax
import jax.numpy as jnp
from jax import lax
from jax.experimental import pallas as pl
from jax.experimental.pallas import tpu as pltpu
from jax.sharding import PartitionSpec as P

MESH = pl.DeviceIdType.MESH
F32 = jnp.float32
BF16 = jnp.bfloat16
NZ = 8


def dot(a, b, dims):
    return lax.dot_general(a, b, (dims, ((), ())), preferred_element_type=F32)


NN = ((1,), (0,))
NT = ((1,), (1,))


def kernel(n, xl, xr, cot, w3, w2t, bias, pair, lg, rg, wg,
           l1, lp, ltf, lt, ltt, rbuf, rt, dbuf, obuf, cbd, gtf, gsend, grecv, hsend, hrecv,
           g2send, g2recv, wsend, wrecv, w1send, zrecv, w2send, wall, wacc, ssem, rsem):
    NR, NC, NS, NZ = n
    NYH = NC // NZ
    NA = NR * NS
    NP = NR * NYH * NS
    SB = xl.shape[1]
    I, J, CP = cot.shape
    JP = xl.shape[2] // 2
    NER = xr.shape[0]
    NE = NER * NR
    C = 2 * NC
    S = SB * NS
    IB = 8
    WR = (NE * C) // NP

    r = lax.axis_index("row")
    c = lax.axis_index("col")
    s = lax.axis_index("seq")
    z = lax.rem(c, NZ)
    yh = lax.div(c, NZ)
    ia = r * NS + s
    ip = (r * NYH + yh) * NS + s

    def seq_peer(k):
        return (r, c, lax.rem(s + k, NS))

    def row_seq_peer(k):
        t = lax.rem(ia + k, NA)
        return (lax.div(t, NS), c, lax.rem(t, NS))

    def col_peer(k):
        return (r, lax.rem(c + k, NC), s)

    def plane_index(k):
        return lax.rem(ip + k, NP)

    def plane_peer(k):
        t = plane_index(k)
        return (lax.div(t, NYH * NS), lax.rem(lax.div(t, NS), NYH) * NZ + z, lax.rem(t, NS))

    def z_peer(k):
        return (r, yh * NZ + lax.rem(z + k, NZ), s)

    def loop(lo, hi, f):
        def step(k, carry):
            f(k)
            return carry
        lax.fori_loop(lo, hi, step, 0)

    def send(src, dst, phase, dev):
        pltpu.make_async_remote_copy(
            src_ref=src, dst_ref=dst, send_sem=ssem.at[phase], recv_sem=rsem.at[phase],
            device_id=dev, device_id_type=MESH,
        ).start()

    def wait_recv(ref, phase):
        pltpu.make_async_copy(ref, ref, rsem.at[phase]).wait()

    def wait_send(ref, phase):
        pltpu.make_async_copy(ref, ref, ssem.at[phase]).wait()

    barrier = pltpu.get_barrier_semaphore()

    def greet(dev):
        pl.semaphore_signal(barrier, inc=1, device_id=dev, device_id_type=MESH)

    loop(1, NP, lambda k: greet(plane_peer(k)))
    loop(1, NZ, lambda k: greet(col_peer(k)))
    loop(NZ + 1, NC, lambda k: greet(col_peer(k)))
    pl.semaphore_wait(barrier, NP - 1 + NC - NYH)

    srow = pl.multiple_of(s * SB, SB)
    erow = pl.multiple_of(r * NER, NER)

    loop(1, NS, lambda k: send(xl.at[lax.rem(s + k, NS)], l1.at[pl.ds(srow, SB)], 0, seq_peer(k)))
    loop(1, NA, lambda k: send(xr, rbuf.at[pl.ds(erow, NER), pl.ds(srow, SB)], 1, row_seq_peer(k)))
    l1[pl.ds(srow, SB), :] = xl[s]
    rbuf[pl.ds(erow, NER), pl.ds(srow, SB), :] = xr[...]
    wait_recv(l1.at[pl.ds(0, (NS - 1) * SB)], 0)

    x = l1[...].astype(F32).T
    lp[c, pl.ds(0, I), :] = x[0:I].astype(BF16)
    lp[c, pl.ds(I, I), :] = x[JP:JP + I].astype(BF16)
    loop(1, NC, lambda k: send(lp.at[c], lp.at[c], 2, col_peer(k)))

    def d_step(k):
        zero = jnp.zeros((JP, CP), BF16)
        for q in range(2):
            i = 2 * k + q
            a = jnp.concatenate([cot[i], jnp.zeros((JP - J, CP), BF16)], axis=0)
            cbd[i, pl.ds(0, JP), :] = jnp.concatenate([a, zero], axis=1)
            cbd[i, pl.ds(JP, JP), :] = jnp.concatenate([zero, a], axis=1)
        rhs = cbd[pl.ds(2 * k, 2)].reshape(4 * JP, 2 * CP)
        d = dot(w3[...], rhs, NT).astype(BF16)
        dbuf[2 * k] = d[:, :2 * JP]
        dbuf[2 * k + 1] = d[:, 2 * JP:]

    loop(0, I // 2, d_step)

    wait_recv(rbuf.at[pl.ds(0, (NE * (NA - 1)) // NA)], 1)
    for e in range(NE):
        rt[pl.ds(e * 2 * JP, 2 * JP), :] = rbuf[e].astype(F32).T.astype(BF16)

    def g_step(k):
        base = k * IB
        lhs = jnp.concatenate(
            [dbuf[pl.ds(base, IB), pl.ds(e * C, C), :].reshape(IB * C, 2 * JP) for e in range(NE)], axis=1
        )
        gtf[pl.ds(pl.multiple_of(base * C, IB * C), IB * C), :] = dot(lhs, rt[...], NN)

    loop(0, I // IB, g_step)
    for q in range(NC):
        for h in range(2):
            gsend[q, pl.ds(h * I, I), :] = gtf[pl.ds(2 * q + h, I, stride=C), :].astype(BF16)
    loop(1, NC, lambda k: send(gsend.at[lax.rem(c + k, NC)], grecv.at[c], 3, col_peer(k)))
    grecv[c] = gsend[c]

    wait_recv(lp.at[pl.ds(0, NC - 1)], 2)
    for q in range(NC):
        for h in range(2):
            ltf[pl.ds(2 * q + h, I, stride=C), :] = lp[q, pl.ds(h * I, I), :].astype(F32)

    def o_step(k):
        base = k * IB
        rows = pl.ds(pl.multiple_of(base * C, IB * C), IB * C)
        a = ltf[rows, :].astype(BF16)
        lt[rows, :] = a
        rhs = jnp.concatenate([rbuf[e] for e in range(NE)], axis=1)
        o = dot(a, rhs, NN).astype(BF16)
        for e in range(NE):
            obuf[pl.ds(base, IB), pl.ds(e * C, C), :] = o[:, e * 2 * JP:(e + 1) * 2 * JP].reshape(IB, C, 2 * JP)

    loop(0, I // IB, o_step)
    wacc[...] = jnp.zeros_like(wacc)

    def w_step(k):
        base = k * IB
        lhs = jnp.concatenate([obuf[base + q] for q in range(IB)], axis=1)
        rhs = cbd[pl.ds(base, IB)].reshape(IB * 2 * JP, 2 * CP)
        wacc[...] += dot(lhs, rhs, NN)

    loop(0, I // IB, w_step)
    for q in range(NP):
        wsend[q] = wacc[pl.ds(q * WR, WR), :].astype(BF16)
    loop(1, NP, lambda k: send(wsend.at[plane_index(k)], wrecv.at[ip], 4, plane_peer(k)))
    wrecv[ip] = wsend[ip]

    for q in range((I * C) // S):
        ltt[:, pl.ds(q * S, S)] = ltf[pl.ds(q * S, S), :].T.astype(BF16)

    def h_step(k):
        rhs = jnp.concatenate(
            [dbuf[:, pl.ds(pl.multiple_of((2 * k + q) * C, C), C), :].reshape(I * C, 2 * JP) for q in range(2)],
            axis=1,
        )
        h = dot(ltt[...], rhs, NN).astype(BF16)
        hsend[2 * k] = h[:, :2 * JP]
        hsend[2 * k + 1] = h[:, 2 * JP:]

    loop(0, NE // 2, h_step)

    def h_piece(t):
        return hsend.at[
            pl.ds(pl.multiple_of(lax.div(t, NS) * NER, NER), NER),
            pl.ds(pl.multiple_of(lax.rem(t, NS) * SB, SB), SB),
        ]

    loop(1, NA, lambda k: send(h_piece(lax.rem(ia + k, NA)), hrecv.at[ia], 5, row_seq_peer(k)))
    hrecv[ia] = hsend[pl.ds(erow, NER), pl.ds(srow, SB), :]

    wait_recv(wrecv.at[pl.ds(0, NP - 1)], 4)
    total = wrecv[0].astype(F32)
    for q in range(1, NP):
        total = total + wrecv[q].astype(F32)
    w1send[...] = total.astype(BF16)
    loop(1, NZ, lambda k: send(w1send, zrecv.at[z], 6, z_peer(k)))
    zrecv[z] = w1send[...]

    def p_step(k):
        rhs = jnp.concatenate([obuf[2 * k], obuf[2 * k + 1]], axis=1)
        y = dot(w2t[...], rhs, NN)
        lo, hi = y[:CP], y[CP:]
        a = lo[:, :2 * JP] + pltpu.roll(hi[:, :2 * JP], JP, 1)
        b = hi[:, 2 * JP:] + pltpu.roll(lo[:, 2 * JP:], JP, 1)
        lane = lax.broadcasted_iota(jnp.int32, a.shape, 1)
        m = jnp.where(lane < JP, a, b).T * (1.0 / S) + bias[...]
        m = m.astype(BF16)
        pair[2 * k] = m[:J]
        pair[2 * k + 1] = m[JP:JP + J]

    loop(0, I // 4, p_step)

    wait_recv(zrecv.at[pl.ds(0, NZ - 1)], 6)
    total = zrecv[0].astype(F32)
    for q in range(1, NZ):
        total = total + zrecv[q].astype(F32)
    w2send[...] = (total * (1.0 / S)).astype(BF16)
    loop(1, NP, lambda k: send(w2send, wall.at[ip], 7, plane_peer(k)))
    wall[ip] = w2send[...]

    loop(I // 4, I // 2, p_step)

    wait_recv(grecv.at[pl.ds(0, NC - 1)], 3)
    total = grecv[0].astype(F32)
    for q in range(1, NC):
        total = total + grecv[q].astype(F32)
    pad = jnp.zeros((JP - I, S), F32)
    t = jnp.concatenate([total[:I], pad, total[I:], pad], axis=0) * (1.0 / S)
    g2send[...] = t.T.astype(BF16)
    loop(1, NS, lambda k: send(
        g2send.at[pl.ds(pl.multiple_of(lax.rem(s + k, NS) * SB, SB), SB)], g2recv.at[s], 8, seq_peer(k)))
    g2recv[s] = g2send[pl.ds(srow, SB), :]

    wait_recv(hrecv.at[pl.ds(0, NA - 1)], 5)
    for e in range(NER):
        total = hrecv[0, e].astype(F32)
        for q in range(1, NA):
            total = total + hrecv[q, e].astype(F32)
        rg[e] = total * (1.0 / S)

    wait_recv(wall.at[pl.ds(0, NP - 1)], 7)
    for q in range(NP):
        wg[pl.ds(q * WR, WR), :] = wall[q]

    wait_recv(g2recv.at[pl.ds(0, NS - 1)], 8)
    lg[...] = g2recv[...].astype(F32)

    wait_send(l1.at[pl.ds(0, (NS - 1) * SB)], 0)
    wait_send(rbuf.at[pl.ds(0, (NE * (NA - 1)) // NA)], 1)
    wait_send(lp.at[pl.ds(0, NC - 1)], 2)
    wait_send(grecv.at[pl.ds(0, NC - 1)], 3)
    wait_send(wrecv.at[pl.ds(0, NP - 1)], 4)
    wait_send(hrecv.at[pl.ds(0, NA - 1)], 5)
    wait_send(zrecv.at[pl.ds(0, NZ - 1)], 6)
    wait_send(wall.at[pl.ds(0, NP - 1)], 7)
    wait_send(g2recv.at[pl.ds(0, NS - 1)], 8)


def body(n, left, right, projection, bias, cotangent):
    NR, NC, NS, NZ = n
    NYH = NC // NZ
    NA = NR * NS
    NP = NR * NYH * NS
    SB = left.shape[0]
    S = SB * NS
    C = 2 * NC
    I, J, CP = cotangent.shape
    JP = -(-J // 64) * 64 if J >= 48 else 2 * J
    NER = right.shape[1] // 2
    NE = NER * NR
    WR = (NE * C) // NP

    xl = left.reshape(SB, 2, NS, I).transpose(2, 0, 1, 3)
    xl = jnp.pad(xl, ((0, 0), (0, 0), (0, 0), (0, JP - I))).reshape(NS, SB, 2 * JP)
    xr = right.reshape(SB, NER, 2, J).transpose(1, 0, 2, 3)
    xr = jnp.pad(xr, ((0, 0), (0, 0), (0, 0), (0, JP - J))).reshape(NER, SB, 2 * JP)
    w3 = projection.reshape(C, NE, 2, CP).transpose(1, 0, 2, 3).reshape(NE * C, 2 * CP)
    w2t = w3.T

    vmem = pl.BlockSpec(memory_space=pltpu.VMEM)
    scratch = [
        pltpu.VMEM((S, 2 * JP), BF16),
        pltpu.VMEM((NC, 2 * I, S), BF16),
        pltpu.VMEM((I * C, S), F32),
        pltpu.VMEM((I * C, S), BF16),
        pltpu.VMEM((S, I * C), BF16),
        pltpu.VMEM((NE, S, 2 * JP), BF16),
        pltpu.VMEM((NE * 2 * JP, S), BF16),
        pltpu.VMEM((I, NE * C, 2 * JP), BF16),
        pltpu.VMEM((I, NE * C, 2 * JP), BF16),
        pltpu.VMEM((I, 2 * JP, 2 * CP), BF16),
        pltpu.VMEM((I * C, S), F32),
        pltpu.VMEM((NC, 2 * I, S), BF16),
        pltpu.VMEM((NC, 2 * I, S), BF16),
        pltpu.VMEM((NE, S, 2 * JP), BF16),
        pltpu.VMEM((NA, NER, SB, 2 * JP), BF16),
        pltpu.VMEM((S, 2 * JP), BF16),
        pltpu.VMEM((NS, SB, 2 * JP), BF16),
        pltpu.VMEM((NP, WR, 2 * CP), BF16),
        pltpu.VMEM((NP, WR, 2 * CP), BF16),
        pltpu.VMEM((WR, 2 * CP), BF16),
        pltpu.VMEM((NZ, WR, 2 * CP), BF16),
        pltpu.VMEM((WR, 2 * CP), BF16),
        pltpu.VMEM((NP, WR, 2 * CP), BF16),
        pltpu.VMEM((NE * C, 2 * CP), F32),
        pltpu.SemaphoreType.DMA((9,)),
        pltpu.SemaphoreType.DMA((9,)),
    ]
    pair, lg, rg, wg = pl.pallas_call(
        functools.partial(kernel, n),
        out_shape=(
            jax.ShapeDtypeStruct((I, J, CP), BF16),
            jax.ShapeDtypeStruct((NS, SB, 2 * JP), F32),
            jax.ShapeDtypeStruct((NER, SB, 2 * JP), F32),
            jax.ShapeDtypeStruct((NE * C, 2 * CP), BF16),
        ),
        in_specs=[vmem] * 6,
        out_specs=(vmem,) * 4,
        scratch_shapes=scratch,
        compiler_params=pltpu.CompilerParams(
            collective_id=0, has_side_effects=True, vmem_limit_bytes=48 * 1024 * 1024
        ),
    )(xl, xr, cotangent, w3, w2t, bias.reshape(1, CP))

    left_grad = lg.reshape(NS, SB, 2, JP)[..., :I].transpose(1, 2, 0, 3).reshape(SB, 2, NS * I)
    right_grad = rg.reshape(NER, SB, 2, JP)[..., :J].transpose(1, 0, 2, 3).reshape(SB, 2 * NER, J)
    weight_grad = wg.reshape(NE, C, 2, CP).transpose(1, 0, 2, 3).reshape(NE * C * 2, CP).astype(F32)
    return pair, left_grad, right_grad, weight_grad


def solution(mesh, nz=NZ):
    n = (mesh.shape["row"], mesh.shape["col"], mesh.shape["seq"], nz)
    return jax.shard_map(
        functools.partial(body, n),
        mesh=mesh,
        in_specs=(
            P("seq", "col", "row"),
            P("seq", "row", "col"),
            P(),
            P(),
            P(("row", "seq"), "col", None),
        ),
        out_specs=(
            P(("row", "seq"), "col", None),
            P("seq", "col", "row"),
            P("seq", "row", "col"),
            P(),
        ),
        check_vma=False,
    )
```

time: 1060 us -> 65.6 us (0.06)
  waiting for transfers between devices: 510 us -> 0 us
  local copies, waits for them, and re-layouts: 269 us -> 7.22 us
  matrix products: 194 us -> 0 us
  Pallas kernels: 0 us -> 57.4 us
  blocking collectives: 50.8 us -> 0 us
  between operations: 13.9 us -> 0.78 us
    psum x1 -> x0, waiting for transfers between devices: 258 us -> none  [body(): weight_grad = lax.psum(grad_w, ('row', 'col', 'seq')) / S]
    reduce_scatter x2 -> x0, waiting for transfers between devices: 233 us -> none  [the longest x1 195 us: body(): lax.psum_scatter(grads_a.astype(jnp.bfloat16), 'col', scatter_dimension=1...]
    dot_general x72 -> x0, matrix products: 194 us -> none  [the longest x12 58.4 us: step(): jnp.einsum('ijce,sci->sej', d_outer, a_blk, preferred_element_type=jnp.fl...]
    convert_element_type x38 -> x2, local copies, waits for them, and re-layouts: 155 us -> 1.34 us  [body(): wg.reshape(NE, C, 2, CP).transpose(1, 0, 2, 3).reshape(NE * C * 2, CP)]
    reshape x12 -> x10, local copies, waits for them, and re-layouts: 86.5 us -> 2.56 us  [the longest x2 0.92 us: body(): xl = left.reshape(SB, 2, NS, I).transpose(2, 0, 1, 3)]
    pallas_call x0 -> x1, Pallas kernels: none -> 57.4 us  [body(): pl.pallas_call(functools.partial(kernel, n), out_shape=(jax.ShapeDtypeStr...]
    all_gather x2 -> x0, blocking collectives: 50.8 us -> none  [the longest x1 41.1 us: body(): a_cols = lax.all_gather(left, 'col', axis=1, tiled=True)]
    unnamed x6 -> x0, waiting for transfers between devices: 19.3 us -> none
  transfers between devices with their start and end apart: 5 -> 0, of which waited for: 4 -> 0; matrix products, arithmetic and copies ran while one was open for 1% -> 0% of each run, Pallas kernels for 0% -> 0%
where the time goes in v1:
time: 65.6 us; the launch traced here: 65.4 us
  Pallas kernels  57.4 us (88%)
  local copies, waits for them, and re-layouts  7.22 us (11%)
  between operations  0.78 us (1%)
    pallas_call x1, Pallas kernels, body(): pl.pallas_call(functools.partial(kernel, n), out_shape=(jax.ShapeDtypeStr...  57.4 us
    unnamed x10, local copies, waits for them, and re-layouts  2.36 us
    convert_element_type x2, local copies, waits for them, and re-layouts, body(): wg.reshape(NE, C, 2, CP).transpose(1, 0, 2, 3).reshape(NE * C * 2, CP)  1.34 us

profile of v1, /device:TPU:1, one launch (start us, length us, event | category | flops | bytes accessed | tf_op | source)
XLA Modules:
  0.0 65.4 jit_solution(10533553872403966143)
XLA Ops:
  0.6 0.9 %reshape.47 = bf16[32,2,4,48]{3,2,1,0:T(4,128)(2,1)S(1)} reshape(bf16[32,2,192]{2,1,0:T(2,128)(2,1)} %param.5) | data formatting | bytes 49152 | tf_op jit(solution)/shard_map/reshape | solution.py:278
  1.5 0.1 copy.29
  1.6 0.0 copy-start.3
  1.6 0.1 pad.7
  1.7 0.0 copy-start.2
  1.7 0.1 reshape.48.xl
  1.8 0.6 copy-done.3
  2.5 0.1 pad.8
  2.5 0.1 reshape.50.xr
  2.6 0.0 copy-done.2
  2.6 0.2 copy.18
  2.9 0.0 copy-start
  2.9 0.1 copy.19
  3.1 0.0 copy-start.1
  3.1 0.9 %copy-done = bf16[48,48,128]{2,1,0:T(8,128)(2,1)S(1)} copy-done((bf16[48,48,128]{2,1,0:T(8,128)(2,1)S(1)}, bf16[48,48,128]{2,1,0:T(8,128)(2,1)}, u32[]{:S(2)}) %copy-start) | copy-done | bytes 589848
  4.0 0.0 copy-done.1
  4.0 57.4 %shard_map.84 = (bf16[48,48,128]{2,1,0:T(8,128)(2,1)S(1)}, f32[4,32,128]{2,1,0:T(8,128)S(1)}, f32[4,32,128]{2,1,0:T(8,128)S(1)}, bf16[512,256]{1,0:T(8,128)(2,1)S(1)}) custom-call(bf16[4,32,128]{2,1,0:T(8,128)(2,1)S(1)} %reshape.48.xl, bf16[4,32,128]{2,1,0:T(8,128)(2,1)S(1)} %reshape.50.xr, bf16[48,48,128]{2,1,0:T(8,128)(2,1)S(1)} %copy-done, ...), custom_call_target="tpu_custom_call" | custom-call | tf_op jit(solution)/shard_map/pallas_call | solution.py:314
  61.3 0.1 reshape.54
  61.5 0.1 copy.20
  61.6 0.8 %reshape.55 = f32[32,2,192]{2,1,0:T(2,128)} reshape(f32[32,2,4,48]{3,2,1,0:T(4,128)S(1)} %copy.20) | data formatting | bytes 98304 | tf_op jit(solution)/shard_map/reshape | solution.py:330
  62.4 0.1 reshape.56
  62.5 0.7 %copy.21 = f32[32,4,2,48]{3,2,1,0:T(2,128)} copy(f32[32,4,2,48]{3,2,0,1:T(2,128)S(1)} %slice_bitcast_fusion) | data formatting | bytes 98304 | tf_op jit(solution)/shard_map/transpose | solution.py:331
  63.2 0.3 reshape.59
  63.5 1.1 %copy.22 = f32[32,16,2,128]{3,2,1,0:T(2,128)} copy(f32[32,16,2,128]{3,2,0,1:T(2,128)S(1)} %bitcast.27) | data formatting | bytes 1048576 | tf_op jit(solution)/shard_map/convert_element_type | solution.py:332
  64.6 0.8 %copy.31 = bf16[48,48,128]{2,1,0:T(8,128)(2,1)} copy(bf16[48,48,128]{2,1,0:T(8,128)(2,1)S(1)} %get-tuple-element.16) | data formatting | bytes 1179648
  (4 shorter events, 0.1 us)
Async XLA Ops:
  1.6 0.8 %copy-start.3 = (bf16[32,8,48]{2,1,0:T(8,128)(2,1)S(1)}, bf16[32,8,48]{2,1,0:T(8,128)(2,1)}, u32[]{:S(2)}) copy-start(bf16[32,8,48]{2,1,0:T(8,128)(2,1)} %param.6) | copy-start | bytes 73732
  1.7 1.0 %copy-start.2 = (bf16[1024,128]{1,0:T(8,128)(2,1)S(1)}, bf16[1024,128]{1,0:T(8,128)(2,1)}, u32[]{:S(2)}) copy-start(bf16[1024,128]{1,0:T(8,128)(2,1)} %param.7) | copy-start | bytes 786436
  2.9 1.1 %copy-start = (bf16[48,48,128]{2,1,0:T(8,128)(2,1)S(1)}, bf16[48,48,128]{2,1,0:T(8,128)(2,1)}, u32[]{:S(2)}) copy-start(bf16[48,48,128]{2,1,0:T(8,128)(2,1)} %cot.1) | copy-start | bytes 1769476
  3.1 0.9 %copy-start.1 = (f32[128]{0:T(128)S(1)}, f32[128]{0:T(128)}, u32[]{:S(2)}) copy-start(f32[128]{0:T(128)} %param.8) | copy-start | bytes 1540

commit v2 on v1

v2 whole, which is shorter than its diff:
```python
import functools

import jax
import jax.numpy as jnp
from jax import lax
from jax.experimental import pallas as pl
from jax.experimental.pallas import tpu as pltpu
from jax.sharding import PartitionSpec as P

MESH = pl.DeviceIdType.MESH
F32 = jnp.float32
BF16 = jnp.bfloat16
NZ = 8


def dot(a, b, dims):
    return lax.dot_general(a, b, (dims, ((), ())), preferred_element_type=F32)


NN = ((1,), (0,))
NT = ((1,), (1,))


def kernel(n, left, right, cot_in, w_in, bias, pair_out, lg, rg, wg,
           leftv, rightv, rightf, cot, wv, wf, w3, w2t, xl, xr,
           lbuf, ltf, ltt, rbuf, rt, dbuf, obuf, cbd, gtf, gsend, grecv, hsend, hrecv,
           g2send, g2recv, wsend, wrecv, w1send, zrecv, w2send, wall, wacc, pair, ssem, rsem, lsem):
    NR, NC, NS, NZ = n
    NYH = NC // NZ
    NA = NR * NS
    NP = NR * NYH * NS
    NL = NC * NS
    SB = xl.shape[1]
    I, J, CP = cot.shape
    JP = xl.shape[2] // 2
    L2 = 2 * JP
    NER = xr.shape[0]
    NE = NER * NR
    C = 2 * NC
    CH = C // 2
    S = SB * NS
    IB = 16

    r = lax.axis_index("row")
    c = lax.axis_index("col")
    s = lax.axis_index("seq")
    z = c % NZ
    yh = c // NZ
    ia = r * NS + s
    ip = (r * NYH + yh) * NS + s
    il = c * NS + s

    def seq_peer(k):
        return (r, c, (s + k) % NS)

    def row_seq_peer(k):
        t = (ia + k) % NA
        return (t // NS, c, t % NS)

    def col_peer(k):
        return (r, (c + k) % NC, s)

    def plane_device(t):
        return (t // (NYH * NS), ((t // NS) % NYH) * NZ + z, t % NS)

    def plane_peer(k):
        return plane_device((ip + k) % NP)

    def z_peer(k):
        return (r, yh * NZ + (z + k) % NZ, s)

    def loop(lo, hi, f):
        def step(k, carry):
            f(k)
            return carry
        lax.fori_loop(lo, hi, step, 0)

    def send(src, dst, phase, dev):
        pltpu.make_async_remote_copy(
            src_ref=src, dst_ref=dst, send_sem=ssem.at[phase], recv_sem=rsem.at[phase],
            device_id=dev, device_id_type=MESH,
        ).start()

    def wait_recv(ref, phase):
        pltpu.make_async_copy(ref, ref, rsem.at[phase]).wait()

    def wait_send(ref, phase):
        pltpu.make_async_copy(ref, ref, ssem.at[phase]).wait()

    loads = [
        pltpu.make_async_copy(src, dst, lsem.at[q])
        for q, (src, dst) in enumerate([(left, leftv), (right, rightv), (w_in, wv), (cot_in, cot)])
    ]
    for load in loads:
        load.start()

    barrier = pltpu.get_barrier_semaphore()

    def greet(dev):
        pl.semaphore_signal(barrier, inc=1, device_id=dev, device_id_type=MESH)

    def greet_row(k):
        t = (il + k) % NL
        greet((r, t // NS, t % NS))

    def greet_plane(k):
        t = (yh * NS + s + k) % (NYH * NS)
        q = k // (NYH * NS)
        greet(((r + q) % NR, (t // NS) * NZ + z, t % NS))

    loop(1, NL, greet_row)
    loop(NYH * NS, NP, greet_plane)

    loads[0].wait()
    loads[1].wait()
    lf = leftv[...].astype(F32)
    zero = jnp.zeros((SB, JP - I), F32)
    for q in range(NS):
        parts = []
        for h in range(2):
            parts += [lf[:, h, q * I:(q + 1) * I], zero]
        xl[q] = jnp.concatenate(parts, axis=1).astype(BF16)
    rightf[:, pl.ds(0, J)] = rightv[...].astype(F32).reshape(SB * 2 * NER, J)
    for e in range(NER):
        parts = []
        for h in range(2):
            parts += [rightf[pl.ds(2 * e + h, SB, stride=2 * NER), :][:, :J], zero]
        xr[e] = jnp.concatenate(parts, axis=1).astype(BF16)

    srow = pl.multiple_of(s * SB, SB)
    erow = pl.multiple_of(r * NER, NER)

    pl.semaphore_wait(barrier, NL - 1 + NP - NYH * NS)

    def send_left(half, k, phase):
        t = (z * NS + s + k) % (NZ * NS)
        send(xl.at[t % NS], lbuf.at[c, pl.ds(srow, SB)], phase, (r, half * NZ + t // NS, t % NS))

    loop(1, NZ * NS, lambda k: send_left(yh, k, 0))
    loop(1, NA, lambda k: send(xr, rbuf.at[pl.ds(erow, NER), pl.ds(srow, SB)], 1, row_seq_peer(k)))
    loop(0, NZ * NS, lambda k: send_left(1 - yh, k, 2))
    lbuf[c, pl.ds(srow, SB), :] = xl[s]
    rbuf[pl.ds(erow, NER), pl.ds(srow, SB), :] = xr[...]

    loads[2].wait()
    loads[3].wait()
    wf[...] = wv[...].astype(F32)
    for ah in range(2):
        for e in range(NE):
            for h in range(2):
                w3[pl.ds((ah * NE + e) * CH, CH), pl.ds(h * CP, CP)] = (
                    wf[pl.ds(ah * CH * 2 * NE + 2 * e + h, CH, stride=2 * NE), :].astype(BF16)
                )
    w2t[...] = w3[...].astype(F32).T.astype(BF16)

    def d_step(k):
        zc = jnp.zeros((JP, CP), BF16)
        for q in range(2):
            i = 2 * k + q
            a = jnp.concatenate([cot[i], jnp.zeros((JP - J, CP), BF16)], axis=0)
            cbd[i, pl.ds(0, JP), :] = jnp.concatenate([a, zc], axis=1)
            cbd[i, pl.ds(JP, JP), :] = jnp.concatenate([zc, a], axis=1)
        rhs = cbd[pl.ds(2 * k, 2)].reshape(2 * L2, 2 * CP)
        d = dot(w3[...], rhs, NT).astype(BF16)
        dbuf[2 * k] = d[:, :L2].reshape(2, NE, CH, L2)
        dbuf[2 * k + 1] = d[:, L2:].reshape(2, NE, CH, L2)

    loop(0, I // 2, d_step)

    wait_recv(rbuf.at[pl.ds(0, (NE * (NA - 1)) // NA)], 1)
    for e in range(NE):
        rt[pl.ds(e * L2, L2), :] = rbuf[e].astype(F32).T.astype(BF16)

    def g_step(k):
        base = k * 8
        lhs = jnp.concatenate(
            [dbuf[pl.ds(base, 8), :, e].reshape(8 * C, L2) for e in range(NE)], axis=1
        )
        gtf[pl.ds(pl.multiple_of(base * C, 8 * C), 8 * C), :] = dot(lhs, rt[...], NN)

    loop(0, I // 8, g_step)
    for q in range(NC):
        for h in range(2):
            gsend[q, pl.ds(h * I, I), :] = gtf[pl.ds(2 * q + h, I, stride=C), :].astype(BF16)

    def half_step(ah):
        lh = ltf.at[ah]
        for q in range(NZ):
            x = lbuf[ah * NZ + q].astype(F32).T
            for h in range(2):
                lh[pl.ds(2 * q + h, I, stride=CH), :] = x[h * JP:h * JP + I]

        def o_step(k):
            base = k * IB
            a = lh[pl.ds(pl.multiple_of(base * CH, IB * CH), IB * CH), :].astype(BF16)
            rhs = jnp.concatenate([rbuf[e] for e in range(NE)], axis=1)
            o = dot(a, rhs, NN).astype(BF16)
            for e in range(NE):
                obuf[pl.ds(base, IB), ah, e] = o[:, e * L2:(e + 1) * L2].reshape(IB, CH, L2)

        loop(0, I // IB, o_step)
        wacc[...] = jnp.zeros_like(wacc)

        def w_step(k):
            base = k * 8
            lhs = jnp.concatenate([obuf[base + q, ah].reshape(NE * CH, L2) for q in range(8)], axis=1)
            wacc[...] += dot(lhs, cbd[pl.ds(base, 8)].reshape(8 * L2, 2 * CP), NN)

        loop(0, I // 8, w_step)
        for e in range(NE):
            wsend[2 * e + ah] = wacc[pl.ds(e * CH, CH), :].astype(BF16)

        def send_piece(k):
            t = 2 * ((ip // 2 + k) % NE) + ah

            @pl.when(t != ip)
            def _():
                send(wsend.at[t], wrecv.at[ip], 4, plane_device(t))

        loop(0, NE, send_piece)

    wait_recv(gtf.at[pl.ds(0, (NZ * NS - 1) * SB // 2)], 0)
    half_step(yh)
    wait_recv(lbuf.at[pl.ds(0, NZ)], 2)
    half_step(1 - yh)
    wrecv[ip] = wsend[ip]
    loop(1, NC, lambda k: send(gsend.at[(c + k) % NC], grecv.at[c], 3, col_peer(k)))
    grecv[c] = gsend[c]

    for ah in range(2):
        for q in range((I * CH) // S):
            ltt[:, pl.ds((ah * I * CH) + q * S, S)] = ltf[ah, pl.ds(q * S, S), :].T.astype(BF16)

    def h_step(k):
        rhs = jnp.concatenate(
            [
                jnp.concatenate([dbuf[:, ah, 2 * k + q].reshape(I * CH, L2) for ah in range(2)], axis=0)
                for q in range(2)
            ],
            axis=1,
        )
        h = dot(ltt[...], rhs, NN).astype(BF16)
        hsend[2 * k] = h[:, :L2]
        hsend[2 * k + 1] = h[:, L2:]

    loop(0, NE // 2, h_step)

    wait_recv(wrecv.at[pl.ds(0, NP - 1)], 4)
    total = wrecv[0].astype(F32)
    for q in range(1, NP):
        total = total + wrecv[q].astype(F32)
    w1send[...] = total.astype(BF16)
    loop(1, NZ, lambda k: send(w1send, zrecv.at[z], 6, z_peer(k)))
    zrecv[z] = w1send[...]

    def h_piece(t):
        return hsend.at[
            pl.ds(pl.multiple_of((t // NS) * NER, NER), NER),
            pl.ds(pl.multiple_of((t % NS) * SB, SB), SB),
        ]

    loop(1, NA, lambda k: send(h_piece((ia + k) % NA), hrecv.at[ia], 5, row_seq_peer(k)))
    hrecv[ia] = hsend[pl.ds(erow, NER), pl.ds(srow, SB), :]

    def p_step(k):
        rhs = jnp.concatenate(
            [obuf[2 * k].reshape(NE * C, L2), obuf[2 * k + 1].reshape(NE * C, L2)], axis=1
        )
        y = dot(w2t[...], rhs, NN)
        lo, hi = y[:CP], y[CP:]
        a = lo[:, :L2] + pltpu.roll(hi[:, :L2], JP, 1)
        b = hi[:, L2:] + pltpu.roll(lo[:, L2:], JP, 1)
        lane = lax.broadcasted_iota(jnp.int32, a.shape, 1)
        m = jnp.where(lane < JP, a, b).T * (1.0 / S) + bias[...]
        m = m.astype(BF16)
        pair[2 * k] = m[:J]
        pair[2 * k + 1] = m[JP:JP + J]

    loop(0, I // 4, p_step)

    wait_recv(zrecv.at[pl.ds(0, NZ - 1)], 6)
    total = zrecv[0].astype(F32)
    for q in range(1, NZ):
        total = total + zrecv[q].astype(F32)
    w2send[...] = (total * (1.0 / S)).astype(BF16)
    loop(1, NP, lambda k: send(w2send, wall.at[ip], 7, plane_peer(k)))
    wall[ip] = w2send[...]

    loop(I // 4, I // 2, p_step)
    store = pltpu.make_async_copy(pair, pair_out, lsem.at[4])
    store.start()

    wait_recv(grecv.at[pl.ds(0, NC - 1)], 3)
    total = grecv[0].astype(F32)
    for q in range(1, NC):
        total = total + grecv[q].astype(F32)
    pad = jnp.zeros((JP - I, S), F32)
    t = jnp.concatenate([total[:I], pad, total[I:], pad], axis=0) * (1.0 / S)
    g2send[...] = t.T.astype(BF16)
    loop(1, NS, lambda k: send(
        g2send.at[pl.ds(pl.multiple_of(((s + k) % NS) * SB, SB), SB)], g2recv.at[s], 8, seq_peer(k)))
    g2recv[s] = g2send[pl.ds(srow, SB), :]

    wait_recv(hrecv.at[pl.ds(0, NA - 1)], 5)
    for e in range(NER):
        total = hrecv[0, e].astype(F32)
        for q in range(1, NA):
            total = total + hrecv[q, e].astype(F32)
        total = total * (1.0 / S)
        for h in range(2):
            rg[:, 2 * e + h, :] = total[:, h * JP:h * JP + J]

    wait_recv(g2recv.at[pl.ds(0, NS - 1)], 8)
    for h in range(2):
        lg[:, h, :] = jnp.concatenate(
            [g2recv[q].astype(F32)[:, h * JP:h * JP + I] for q in range(NS)], axis=1
        )

    wait_recv(wall.at[pl.ds(0, NP - 1)], 7)
    for ah in range(2):
        for e in range(NE):
            x = wall[2 * e + ah].astype(F32)
            for h in range(2):
                wg[pl.ds(ah * CH * 2 * NE + 2 * e + h, CH, stride=2 * NE), :] = x[:, h * CP:(h + 1) * CP]

    wait_send(gtf.at[pl.ds(0, (NZ * NS - 1) * SB // 2)], 0)
    wait_send(rbuf.at[pl.ds(0, (NE * (NA - 1)) // NA)], 1)
    wait_send(lbuf.at[pl.ds(0, NZ)], 2)
    wait_send(grecv.at[pl.ds(0, NC - 1)], 3)
    wait_send(wrecv.at[pl.ds(0, NP - 1)], 4)
    wait_send(hrecv.at[pl.ds(0, NA - 1)], 5)
    wait_send(zrecv.at[pl.ds(0, NZ - 1)], 6)
    wait_send(wall.at[pl.ds(0, NP - 1)], 7)
    wait_send(g2recv.at[pl.ds(0, NS - 1)], 8)
    store.wait()


def body(n, left, right, projection, bias, cotangent):
    NR, NC, NS, NZ = n
    NYH = NC // NZ
    NA = NR * NS
    NP = NR * NYH * NS
    SB = left.shape[0]
    S = SB * NS
    C = 2 * NC
    CH = C // 2
    I, J, CP = cotangent.shape
    JP = 64 if J == 48 else 2 * J
    L2 = 2 * JP
    NER = right.shape[1] // 2
    NE = NER * NR

    vmem = pl.BlockSpec(memory_space=pltpu.VMEM)
    hbm = pl.BlockSpec(memory_space=pl.ANY)
    scratch = [
        pltpu.VMEM(left.shape, BF16),
        pltpu.VMEM(right.shape, BF16),
        pltpu.VMEM((SB * 2 * NER, 128), F32),
        pltpu.VMEM(cotangent.shape, BF16),
        pltpu.VMEM(projection.shape, BF16),
        pltpu.VMEM(projection.shape, F32),
        pltpu.VMEM((NE * C, 2 * CP), BF16),
        pltpu.VMEM((2 * CP, NE * C), BF16),
        pltpu.VMEM((NS, SB, L2), BF16),
        pltpu.VMEM((NER, SB, L2), BF16),
        pltpu.VMEM((NC, S, L2), BF16),
        pltpu.VMEM((2, I * CH, S), F32),
        pltpu.VMEM((S, I * C), BF16),
        pltpu.VMEM((NE, S, L2), BF16),
        pltpu.VMEM((NE * L2, S), BF16),
        pltpu.VMEM((I, 2, NE, CH, L2), BF16),
        pltpu.VMEM((I, 2, NE, CH, L2), BF16),
        pltpu.VMEM((I, L2, 2 * CP), BF16),
        pltpu.VMEM((I * C, S), F32),
        pltpu.VMEM((NC, 2 * I, S), BF16),
        pltpu.VMEM((NC, 2 * I, S), BF16),
        pltpu.VMEM((NE, S, L2), BF16),
        pltpu.VMEM((NA, NER, SB, L2), BF16),
        pltpu.VMEM((S, L2), BF16),
        pltpu.VMEM((NS, SB, L2), BF16),
        pltpu.VMEM((NP, CH, 2 * CP), BF16),
        pltpu.VMEM((NP, CH, 2 * CP), BF16),
        pltpu.VMEM((CH, 2 * CP), BF16),
        pltpu.VMEM((NZ, CH, 2 * CP), BF16),
        pltpu.VMEM((CH, 2 * CP), BF16),
        pltpu.VMEM((NP, CH, 2 * CP), BF16),
        pltpu.VMEM((NE * CH, 2 * CP), F32),
        pltpu.VMEM((I, J, CP), BF16),
        pltpu.SemaphoreType.DMA((9,)),
        pltpu.SemaphoreType.DMA((9,)),
        pltpu.SemaphoreType.DMA((5,)),
    ]
    return pl.pallas_call(
        functools.partial(kernel, n),
        out_shape=(
            jax.ShapeDtypeStruct((I, J, CP), BF16),
            jax.ShapeDtypeStruct(left.shape, F32),
            jax.ShapeDtypeStruct(right.shape, F32),
            jax.ShapeDtypeStruct(projection.shape, F32),
        ),
        in_specs=[hbm] * 4 + [vmem],
        out_specs=(hbm, vmem, vmem, vmem),
        scratch_shapes=scratch,
        compiler_params=pltpu.CompilerParams(
            collective_id=0, has_side_effects=True, vmem_limit_bytes=60 * 1024 * 1024
        ),
    )(left, right, cotangent, projection, bias.reshape(1, CP))


def solution(mesh, nz=NZ):
    n = (mesh.shape["row"], mesh.shape["col"], mesh.shape["seq"], nz)
    return jax.shard_map(
        functools.partial(body, n),
        mesh=mesh,
        in_specs=(
            P("seq", "col", "row"),
            P("seq", "row", "col"),
            P(),
            P(),
            P(("row", "seq"), "col", None),
        ),
        out_specs=(
            P(("row", "seq"), "col", None),
            P("seq", "col", "row"),
            P("seq", "row", "col"),
            P(),
        ),
        check_vma=False,
    )
```

time: 65.6 us -> 63.9 us (0.974)
  local copies, waits for them, and re-layouts: 7.22 us -> 4.36 us
  Pallas kernels: 57.4 us -> 58.8 us
    reshape x10 -> x0, local copies, waits for them, and re-layouts: 2.56 us -> none  [the longest x2 0.92 us: body(): xl = left.reshape(SB, 2, NS, I).transpose(2, 0, 1, 3)]
    unnamed x10, local copies, waits for them, and re-layouts: 2.36 us -> 4.36 us
    pallas_call x1, Pallas kernels: 57.4 us -> 58.8 us  [body(): pl.pallas_call(functools.partial(kernel, n), out_shape=(jax.ShapeDtypeStr...]
    convert_element_type x2 -> x0, local copies, waits for them, and re-layouts: 1.34 us -> none  [body(): wg.reshape(NE, C, 2, CP).transpose(1, 0, 2, 3).reshape(NE * C * 2, CP)]
    transpose x4 -> x0, local copies, waits for them, and re-layouts: 0.81 us -> none  [the longest x2 0.71 us: body(): rg.reshape(NER, SB, 2, JP)[..., :J].transpose(1, 0, 2, 3)]
where the time goes in v2:
time: 63.9 us; the launch traced here: 63.8 us
  Pallas kernels  58.8 us (92%)
  local copies, waits for them, and re-layouts  4.36 us (7%)
  between operations  0.66 us (1%)
    pallas_call x1, Pallas kernels, body(): pl.pallas_call(functools.partial(kernel, n), out_shape=(jax.ShapeDtypeStr...  58.8 us
    unnamed x10, local copies, waits for them, and re-layouts  4.36 us

profile of v2, /device:TPU:1, one launch (start us, length us, event | category | flops | bytes accessed | tf_op | source)
XLA Modules:
  0.0 63.8 jit_solution(9248739322582723305)
XLA Ops:
  0.6 58.8 %shard_map.84 = (bf16[48,48,128]{2,1,0:T(8,128)(2,1)}, f32[32,2,192]{2,1,0:T(2,128)}, f32[32,8,48]{2,1,0:T(8,128)}, f32[1024,128]{1,0:T(8,128)}) custom-call(bf16[32,2,192]{2,1,0:T(2,128)(2,1)} %left.1, bf16[32,8,48]{2,1,0:T(8,128)(2,1)} %right.1, bf16[48,48,128]{2,1,0:T(8,128)(2,1)} %cot_in.1, bf16[1024,128]{1,0:T(8,128)(2,1)} %w_in.1, f32[1,128]{1,0:T(1,128)} %bitcast.1), custom_call_target="tpu_custom_call" | custom-call | tf_op jit(solution)/shard_map/pallas_call | solution.py:393
  59.4 0.0 copy-start.2
  59.4 0.0 copy-start
  59.4 2.0 %copy.13 = bf16[48,48,128]{2,1,0:T(8,128)(2,1)} copy(bf16[48,48,128]{2,1,0:T(8,128)(2,1)} %get-tuple-element.8) | data formatting | bytes 1179648
  61.4 0.0 copy-done.2
  61.4 0.0 copy-start.1
  61.4 0.6 copy.14
  62.0 0.3 copy-done.1
  62.3 0.7 %copy.15 = f32[32,8,48]{2,1,0:T(8,128)} copy(f32[32,8,48]{2,1,0:T(8,128)S(1)} %copy-done.1) | data formatting | bytes 98304
  63.0 0.0 copy-done
  63.0 0.8 %copy.16 = f32[1024,128]{1,0:T(8,128)} copy(f32[1024,128]{1,0:T(8,128)S(1)} %copy-done) | data formatting | bytes 1048576
Async XLA Ops:
  59.4 2.0 %copy-start.2 = (f32[32,2,192]{2,1,0:T(2,128)S(1)}, f32[32,2,192]{2,1,0:T(2,128)}, u32[]{:S(2)}) copy-start(f32[32,2,192]{2,1,0:T(2,128)} %get-tuple-element.9) | copy-start | bytes 147460
  59.4 3.6 %copy-start = (f32[1024,128]{1,0:T(8,128)S(1)}, f32[1024,128]{1,0:T(8,128)}, u32[]{:S(2)}) copy-start(f32[1024,128]{1,0:T(8,128)} %get-tuple-element.11) | copy-start | bytes 1572868
  61.4 0.9 %copy-start.1 = (f32[32,8,48]{2,1,0:T(8,128)S(1)}, f32[32,8,48]{2,1,0:T(8,128)}, u32[]{:S(2)}) copy-start(f32[32,8,48]{2,1,0:T(8,128)} %get-tuple-element.10) | copy-start | bytes 147460

commit v3 on v2

--- a/solution.py
+++ b/solution.py
@@ -1,4 +1,5 @@
 import functools
+import math
 
 import jax
 import jax.numpy as jnp
@@ -17,19 +18,22 @@
     return lax.dot_general(a, b, (dims, ((), ())), preferred_element_type=F32)
 
 
+def log2(size):
+    return size.bit_length() - 1
+
+
 NN = ((1,), (0,))
 NT = ((1,), (1,))
 
 
-def kernel(n, left, right, cot_in, w_in, bias, pair_out, lg, rg, wg,
+def kernel(n, left, right, cot_in, w_in, bias, pair, lg, rg, wg,
            leftv, rightv, rightf, cot, wv, wf, w3, w2t, xl, xr,
            lbuf, ltf, ltt, rbuf, rt, dbuf, obuf, cbd, gtf, gsend, grecv, hsend, hrecv,
-           g2send, g2recv, wsend, wrecv, w1send, zrecv, w2send, wall, wacc, pair, ssem, rsem, lsem):
+           g2send, g2recv, wsend, wrecv, w1send, zrecv, w2send, wall, wacc, ssem, rsem, lsem):
     NR, NC, NS, NZ = n
     NYH = NC // NZ
     NA = NR * NS
     NP = NR * NYH * NS
-    NL = NC * NS
     SB = xl.shape[1]
     I, J, CP = cot.shape
     JP = xl.shape[2] // 2
@@ -39,41 +43,43 @@
     C = 2 * NC
     CH = C // 2
     S = SB * NS
-    IB = 16
+    IB = I
 
     r = lax.axis_index("row")
     c = lax.axis_index("col")
     s = lax.axis_index("seq")
-    z = c % NZ
+    z = c & (NZ - 1)
     yh = c // NZ
     ia = r * NS + s
     ip = (r * NYH + yh) * NS + s
-    il = c * NS + s
 
     def seq_peer(k):
-        return (r, c, (s + k) % NS)
+        return (r, c, (s + k) & (NS - 1))
 
     def row_seq_peer(k):
-        t = (ia + k) % NA
-        return (t // NS, c, t % NS)
+        t = (ia + k) & (NA - 1)
+        return (t >> log2(NS), c, t & (NS - 1))
 
     def col_peer(k):
-        return (r, (c + k) % NC, s)
+        return (r, (c + k) & (NC - 1), s)
 
     def plane_device(t):
-        return (t // (NYH * NS), ((t // NS) % NYH) * NZ + z, t % NS)
+        return (t >> log2(NYH * NS), ((t >> log2(NS)) & (NYH - 1)) * NZ + z, t & (NS - 1))
 
     def plane_peer(k):
-        return plane_device((ip + k) % NP)
+        return plane_device((ip + k) & (NP - 1))
 
     def z_peer(k):
-        return (r, yh * NZ + (z + k) % NZ, s)
-
-    def loop(lo, hi, f):
+        return (r, yh * NZ + ((z + k) & (NZ - 1)), s)
+
+    def loop(lo, hi, f, unroll=1):
+        unroll = math.gcd(hi - lo, unroll)
+
         def step(k, carry):
-            f(k)
+            for q in range(unroll):
+                f(lo + k * unroll + q)
             return carry
-        lax.fori_loop(lo, hi, step, 0)
+        lax.fori_loop(0, (hi - lo) // unroll, step, 0)
 
     def send(src, dst, phase, dev):
         pltpu.make_async_remote_copy(
@@ -99,17 +105,19 @@
     def greet(dev):
         pl.semaphore_signal(barrier, inc=1, device_id=dev, device_id_type=MESH)
 
+    def greet_col(k):
+        for t in range(NS):
+            greet((r, (c + k) & (NC - 1), t))
+
     def greet_row(k):
-        t = (il + k) % NL
-        greet((r, t // NS, t % NS))
-
-    def greet_plane(k):
-        t = (yh * NS + s + k) % (NYH * NS)
-        q = k // (NYH * NS)
-        greet(((r + q) % NR, (t // NS) * NZ + z, t % NS))
-
-    loop(1, NL, greet_row)
-    loop(NYH * NS, NP, greet_plane)
+        for h in range(NYH):
+            for t in range(NS):
+                greet(((r + k) & (NR - 1), h * NZ + z, t))
+
+    loop(1, NR, greet_row)
+    loop(1, NC, greet_col)
+    for k in range(1, NS):
+        greet(seq_peer(k))
 
     loads[0].wait()
     loads[1].wait()
@@ -130,15 +138,23 @@
     srow = pl.multiple_of(s * SB, SB)
     erow = pl.multiple_of(r * NER, NER)
 
-    pl.semaphore_wait(barrier, NL - 1 + NP - NYH * NS)
+    pl.semaphore_wait(barrier, NC * NS - 1 + NP - NYH * NS)
 
     def send_left(half, k, phase):
-        t = (z * NS + s + k) % (NZ * NS)
-        send(xl.at[t % NS], lbuf.at[c, pl.ds(srow, SB)], phase, (r, half * NZ + t // NS, t % NS))
-
-    loop(1, NZ * NS, lambda k: send_left(yh, k, 0))
-    loop(1, NA, lambda k: send(xr, rbuf.at[pl.ds(erow, NER), pl.ds(srow, SB)], 1, row_seq_peer(k)))
-    loop(0, NZ * NS, lambda k: send_left(1 - yh, k, 2))
+        for t in range(NS):
+            send(xl.at[t], lbuf.at[c, pl.ds(srow, SB)], phase, (r, half * NZ + ((z + k) & (NZ - 1)), t))
+
+    def send_right(k):
+        for t in range(NS):
+            send(xr, rbuf.at[pl.ds(erow, NER), pl.ds(srow, SB)], 1, ((r + k) & (NR - 1), c, t))
+
+    loop(1, NR, send_right)
+    for k in range(1, NS):
+        send(xr, rbuf.at[pl.ds(erow, NER), pl.ds(srow, SB)], 1, seq_peer(k))
+    for k in range(1, NS):
+        send(xl.at[(s + k) & (NS - 1)], lbuf.at[c, pl.ds(srow, SB)], 0, seq_peer(k))
+    loop(1, NZ, lambda k: send_left(yh, k, 0))
+    loop(0, NZ, lambda k: send_left(1 - yh, k, 2))
     lbuf[c, pl.ds(srow, SB), :] = xl[s]
     rbuf[pl.ds(erow, NER), pl.ds(srow, SB), :] = xr[...]
 
@@ -165,7 +181,7 @@
         dbuf[2 * k] = d[:, :L2].reshape(2, NE, CH, L2)
         dbuf[2 * k + 1] = d[:, L2:].reshape(2, NE, CH, L2)
 
-    loop(0, I // 2, d_step)
+    loop(0, I // 2, d_step, 4)
 
     wait_recv(rbuf.at[pl.ds(0, (NE * (NA - 1)) // NA)], 1)
     for e in range(NE):
@@ -178,7 +194,7 @@
         )
         gtf[pl.ds(pl.multiple_of(base * C, 8 * C), 8 * C), :] = dot(lhs, rt[...], NN)
 
-    loop(0, I // 8, g_step)
+    loop(0, I // 8, g_step, 3)
     for q in range(NC):
         for h in range(2):
             gsend[q, pl.ds(h * I, I), :] = gtf[pl.ds(2 * q + h, I, stride=C), :].astype(BF16)
@@ -206,12 +222,12 @@
             lhs = jnp.concatenate([obuf[base + q, ah].reshape(NE * CH, L2) for q in range(8)], axis=1)
             wacc[...] += dot(lhs, cbd[pl.ds(base, 8)].reshape(8 * L2, 2 * CP), NN)
 
-        loop(0, I // 8, w_step)
+        loop(0, I // 8, w_step, 3)
         for e in range(NE):
             wsend[2 * e + ah] = wacc[pl.ds(e * CH, CH), :].astype(BF16)
 
         def send_piece(k):
-            t = 2 * ((ip // 2 + k) % NE) + ah
+            t = 2 * (((ip >> 1) + k) & (NE - 1)) + ah
 
             @pl.when(t != ip)
             def _():
@@ -222,9 +238,9 @@
     wait_recv(gtf.at[pl.ds(0, (NZ * NS - 1) * SB // 2)], 0)
     half_step(yh)
     wait_recv(lbuf.at[pl.ds(0, NZ)], 2)
+    loop(1, NC, lambda k: send(gsend.at[(c + k) & (NC - 1)], grecv.at[c], 3, col_peer(k)))
     half_step(1 - yh)
     wrecv[ip] = wsend[ip]
-    loop(1, NC, lambda k: send(gsend.at[(c + k) % NC], grecv.at[c], 3, col_peer(k)))
     grecv[c] = gsend[c]
 
     for ah in range(2):
@@ -243,7 +259,7 @@
         hsend[2 * k] = h[:, :L2]
         hsend[2 * k + 1] = h[:, L2:]
 
-    loop(0, NE // 2, h_step)
+    loop(0, NE // 2, h_step, 2)
 
     wait_recv(wrecv.at[pl.ds(0, NP - 1)], 4)
     total = wrecv[0].astype(F32)
@@ -255,11 +271,11 @@
 
     def h_piece(t):
         return hsend.at[
-            pl.ds(pl.multiple_of((t // NS) * NER, NER), NER),
-            pl.ds(pl.multiple_of((t % NS) * SB, SB), SB),
+            pl.ds(pl.multiple_of((t >> log2(NS)) * NER, NER), NER),
+            pl.ds(pl.multiple_of((t & (NS - 1)) * SB, SB), SB),
         ]
 
-    loop(1, NA, lambda k: send(h_piece((ia + k) % NA), hrecv.at[ia], 5, row_seq_peer(k)))
+    loop(1, NA, lambda k: send(h_piece((ia + k) & (NA - 1)), hrecv.at[ia], 5, row_seq_peer(k)))
     hrecv[ia] = hsend[pl.ds(erow, NER), pl.ds(srow, SB), :]
 
     def p_step(k):
@@ -276,7 +292,7 @@
         pair[2 * k] = m[:J]
         pair[2 * k + 1] = m[JP:JP + J]
 
-    loop(0, I // 4, p_step)
+    loop(0, I // 4, p_step, 4)
 
     wait_recv(zrecv.at[pl.ds(0, NZ - 1)], 6)
     total = zrecv[0].astype(F32)
@@ -285,10 +301,6 @@
     w2send[...] = (total * (1.0 / S)).astype(BF16)
     loop(1, NP, lambda k: send(w2send, wall.at[ip], 7, plane_peer(k)))
     wall[ip] = w2send[...]
-
-    loop(I // 4, I // 2, p_step)
-    store = pltpu.make_async_copy(pair, pair_out, lsem.at[4])
-    store.start()
 
     wait_recv(grecv.at[pl.ds(0, NC - 1)], 3)
     total = grecv[0].astype(F32)
@@ -298,8 +310,10 @@
     t = jnp.concatenate([total[:I], pad, total[I:], pad], axis=0) * (1.0 / S)
     g2send[...] = t.T.astype(BF16)
     loop(1, NS, lambda k: send(
-        g2send.at[pl.ds(pl.multiple_of(((s + k) % NS) * SB, SB), SB)], g2recv.at[s], 8, seq_peer(k)))
+        g2send.at[pl.ds(pl.multiple_of(((s + k) & (NS - 1)) * SB, SB), SB)], g2recv.at[s], 8, seq_peer(k)))
     g2recv[s] = g2send[pl.ds(srow, SB), :]
+
+    loop(I // 4, I // 2, p_step, 4)
 
     wait_recv(hrecv.at[pl.ds(0, NA - 1)], 5)
     for e in range(NER):
@@ -332,7 +346,15 @@
     wait_send(zrecv.at[pl.ds(0, NZ - 1)], 6)
     wait_send(wall.at[pl.ds(0, NP - 1)], 7)
     wait_send(g2recv.at[pl.ds(0, NS - 1)], 8)
-    store.wait()
+
+
+def finish(*refs):
+    sem = refs[8]
+    copies = [pltpu.make_async_copy(refs[q], refs[4 + q], sem.at[q]) for q in range(4)]
+    for copy in copies:
+        copy.start()
+    for copy in copies:
+        copy.wait()
 
 
 def body(n, left, right, projection, bias, cotangent):
@@ -385,26 +407,29 @@
         pltpu.VMEM((CH, 2 * CP), BF16),
         pltpu.VMEM((NP, CH, 2 * CP), BF16),
         pltpu.VMEM((NE * CH, 2 * CP), F32),
-        pltpu.VMEM((I, J, CP), BF16),
         pltpu.SemaphoreType.DMA((9,)),
         pltpu.SemaphoreType.DMA((9,)),
-        pltpu.SemaphoreType.DMA((5,)),
+        pltpu.SemaphoreType.DMA((4,)),
     ]
-    return pl.pallas_call(
+    shapes = ((I, J, CP), BF16), (left.shape, F32), (right.shape, F32), (projection.shape, F32)
+    results = pl.pallas_call(
         functools.partial(kernel, n),
-        out_shape=(
-            jax.ShapeDtypeStruct((I, J, CP), BF16),
-            jax.ShapeDtypeStruct(left.shape, F32),
-            jax.ShapeDtypeStruct(right.shape, F32),
-            jax.ShapeDtypeStruct(projection.shape, F32),
-        ),
+        out_shape=tuple(pltpu.VMEM(shape, dtype) for shape, dtype in shapes),
         in_specs=[hbm] * 4 + [vmem],
-        out_specs=(hbm, vmem, vmem, vmem),
+        out_specs=(vmem,) * 4,
         scratch_shapes=scratch,
         compiler_params=pltpu.CompilerParams(
-            collective_id=0, has_side_effects=True, vmem_limit_bytes=60 * 1024 * 1024
+            collective_id=0, has_side_effects=True, vmem_limit_bytes=62 * 1024 * 1024
         ),
     )(left, right, cotangent, projection, bias.reshape(1, CP))
+    return pl.pallas_call(
+        finish,
+        out_shape=tuple(jax.ShapeDtypeStruct(shape, dtype) for shape, dtype in shapes),
+        in_specs=[vmem] * 4,
+        out_specs=(hbm,) * 4,
+        scratch_shapes=[pltpu.SemaphoreType.DMA((4,))],
+        compiler_params=pltpu.CompilerParams(vmem_limit_bytes=4 * 1024 * 1024),
+    )(*results)
 
 
 def solution(mesh, nz=NZ):

time: 63.9 us -> 52.9 us (0.83)
  Pallas kernels: 58.8 us -> 52.2 us
  local copies, waits for them, and re-layouts: 4.36 us -> 0 us
    pallas_call x1 -> x2, Pallas kernels: 58.8 us -> 52.2 us  [the longest x1 51.1 us: body(): pl.pallas_call(functools.partial(kernel, n), out_shape=tuple((pltpu.VMEM(...]
    unnamed x10 -> x0, local copies, waits for them, and re-layouts: 4.36 us -> none
where the time goes in v3:
time: 52.9 us; the launch traced here: 52.8 us
  Pallas kernels  52.2 us (99%)
  between operations  0.64 us (1%)
    pallas_call x1, Pallas kernels, body(): pl.pallas_call(functools.partial(kernel, n), out_shape=tuple((pltpu.VMEM(...  51.1 us
    pallas_call x1, Pallas kernels, body(): pl.pallas_call(finish, out_shape=tuple((jax.ShapeDtypeStruct(shape, dtype...  1.09 us

profile of v3, /device:TPU:1, one launch (start us, length us, event | category | flops | bytes accessed | tf_op | source)
XLA Modules:
  0.0 52.8 jit_solution(7459193255825566760)
XLA Ops:
  0.6 51.1 %shard_map.84 = (bf16[48,48,128]{2,1,0:T(8,128)(2,1)S(1)}, f32[32,2,192]{2,1,0:T(2,128)S(1)}, f32[32,8,48]{2,1,0:T(8,128)S(1)}, f32[1024,128]{1,0:T(8,128)S(1)}) custom-call(bf16[32,2,192]{2,1,0:T(2,128)(2,1)} %left.1, bf16[32,8,48]{2,1,0:T(8,128)(2,1)} %right.1, bf16[48,48,128]{2,1,0:T(8,128)(2,1)} %cot_in.1, bf16[1024,128]{1,0:T(8,128)(2,1)} %w_in.1, ...), custom_call_target="tpu_custom_call" | custom-call | tf_op jit(solution)/shard_map/pallas_call | solution.py:415
  51.7 1.1 %shard_map.85 = (bf16[48,48,128]{2,1,0:T(8,128)(2,1)}, f32[32,2,192]{2,1,0:T(2,128)}, f32[32,8,48]{2,1,0:T(8,128)}, f32[1024,128]{1,0:T(8,128)}) custom-call(bf16[48,48,128]{2,1,0:T(8,128)(2,1)S(1)} %get-tuple-element.8.refs_0_, f32[32,2,192]{2,1,0:T(2,128)S(1)} %get-tuple-element.9.refs_1_, f32[32,8,48]{2,1,0:T(8,128)S(1)} %get-tuple-element.10.refs_2_, ...), custom_call_target="tpu_custom_call" | custom-call | tf_op jit(solution)/shard_map/pallas_call | solution.py:425

commit v4 on v3

--- a/solution.py
+++ b/solution.py
@@ -26,10 +26,10 @@
 NT = ((1,), (1,))
 
 
-def kernel(n, left, right, cot_in, w_in, bias, pair, lg, rg, wg,
-           leftv, rightv, rightf, cot, wv, wf, w3, w2t, xl, xr,
-           lbuf, ltf, ltt, rbuf, rt, dbuf, obuf, cbd, gtf, gsend, grecv, hsend, hrecv,
-           g2send, g2recv, wsend, wrecv, w1send, zrecv, w2send, wall, wacc, ssem, rsem, lsem):
+def kernel(n, left, right, cot_in, w_in, bias_in, pair, lg, rg, wg,
+           bias, leftv, rightv, rightf, cot, wv, wf, w3, w2t, xl, xr,
+           lbuf, ltf, ltt, rbuf, rt, dbuf, obuf, cbd, gtf, gsend, gx, g1send, grecv, hsend, hx, h1send, hrecv,
+           wsend, wrecv, w1send, zrecv, w2send, wall, wacc, ssem, rsem, nsem, fsem, lsem):
     NR, NC, NS, NZ = n
     NYH = NC // NZ
     NA = NR * NS
@@ -56,13 +56,6 @@
     def seq_peer(k):
         return (r, c, (s + k) & (NS - 1))
 
-    def row_seq_peer(k):
-        t = (ia + k) & (NA - 1)
-        return (t >> log2(NS), c, t & (NS - 1))
-
-    def col_peer(k):
-        return (r, (c + k) & (NC - 1), s)
-
     def plane_device(t):
         return (t >> log2(NYH * NS), ((t >> log2(NS)) & (NYH - 1)) * NZ + z, t & (NS - 1))
 
@@ -95,7 +88,7 @@
 
     loads = [
         pltpu.make_async_copy(src, dst, lsem.at[q])
-        for q, (src, dst) in enumerate([(left, leftv), (right, rightv), (w_in, wv), (cot_in, cot)])
+        for q, (src, dst) in enumerate([(left, leftv), (right, rightv), (w_in, wv), (cot_in, cot), (bias_in, bias)])
     ]
     for load in loads:
         load.start()
@@ -105,9 +98,17 @@
     def greet(dev):
         pl.semaphore_signal(barrier, inc=1, device_id=dev, device_id_type=MESH)
 
-    def greet_col(k):
-        for t in range(NS):
-            greet((r, (c + k) & (NC - 1), t))
+    near = sorted(range(NZ), key=lambda k: min(k, NZ - k))
+    relayed = [k for k in near if min(k, NZ - k) > NZ // 4]
+    direct = [k for k in near if k not in relayed]
+
+    def greet_z(k):
+        t = (z + k) & (NZ - 1)
+        for q in range(NS):
+            greet((r, yh * NZ + t, q))
+        if k in direct:
+            for q in range(NS):
+                greet((r, (1 - yh) * NZ + t, q))
 
     def greet_row(k):
         for h in range(NYH):
@@ -115,9 +116,12 @@
                 greet(((r + k) & (NR - 1), h * NZ + z, t))
 
     loop(1, NR, greet_row)
-    loop(1, NC, greet_col)
+    for k in relayed[::-1] + direct[:0:-1]:
+        greet_z(k)
     for k in range(1, NS):
         greet(seq_peer(k))
+    for q in range(NS):
+        greet((r, (1 - yh) * NZ + z, q))
 
     loads[0].wait()
     loads[1].wait()
@@ -138,28 +142,45 @@
     srow = pl.multiple_of(s * SB, SB)
     erow = pl.multiple_of(r * NER, NER)
 
-    pl.semaphore_wait(barrier, NC * NS - 1 + NP - NYH * NS)
-
-    def send_left(half, k, phase):
+    pl.semaphore_wait(barrier, (NR - 1) * NYH * NS + (NZ - 1) * 2 * NS - len(relayed) * NS + 2 * NS - 1)
+
+    def copy(src, dst, send_sem, recv_sem, dev):
+        pltpu.make_async_remote_copy(
+            src_ref=src, dst_ref=dst, send_sem=send_sem, recv_sem=recv_sem, device_id=dev, device_id_type=MESH
+        ).start()
+
+    core = s & 1
+    sibling = (r, c, s + 1 - 2 * core)
+
+    def right_to(dev):
+        send(xr, rbuf.at[pl.ds(erow, NER), pl.ds(srow, SB)], 1, dev)
+
+    for k in range(1, NR):
+        for t in range(NS // 2):
+            right_to(((r + k) & (NR - 1), c, 2 * t + core))
+    for k in range(1, NS // 2):
+        right_to((r, c, (s + 2 * k) & (NS - 1)))
+
+    def left_to(half, k, send_sem, recv_sem):
         for t in range(NS):
-            send(xl.at[t], lbuf.at[c, pl.ds(srow, SB)], phase, (r, half * NZ + ((z + k) & (NZ - 1)), t))
-
-    def send_right(k):
-        for t in range(NS):
-            send(xr, rbuf.at[pl.ds(erow, NER), pl.ds(srow, SB)], 1, ((r + k) & (NR - 1), c, t))
-
-    loop(1, NR, send_right)
-    for k in range(1, NS):
-        send(xr, rbuf.at[pl.ds(erow, NER), pl.ds(srow, SB)], 1, seq_peer(k))
-    for k in range(1, NS):
-        send(xl.at[(s + k) & (NS - 1)], lbuf.at[c, pl.ds(srow, SB)], 0, seq_peer(k))
-    loop(1, NZ, lambda k: send_left(yh, k, 0))
-    loop(0, NZ, lambda k: send_left(1 - yh, k, 2))
+            copy(xl.at[t], lbuf.at[c, pl.ds(srow, SB)], send_sem, recv_sem,
+                 (r, half * NZ + ((z + k) & (NZ - 1)), t))
+
+    arrival = relayed[::-1] + direct
+    for k in arrival:
+        if k == 0:
+            for t in range(1, NS):
+                copy(xl.at[(s + t) & (NS - 1)], lbuf.at[c, pl.ds(srow, SB)], ssem.at[0], nsem.at[0], seq_peer(t))
+        else:
+            left_to(yh, k, ssem.at[0], nsem.at[k])
+    for k in direct:
+        left_to(1 - yh, k, ssem.at[2], fsem.at[k])
     lbuf[c, pl.ds(srow, SB), :] = xl[s]
     rbuf[pl.ds(erow, NER), pl.ds(srow, SB), :] = xr[...]
 
     loads[2].wait()
     loads[3].wait()
+    loads[4].wait()
     wf[...] = wv[...].astype(F32)
     for ah in range(2):
         for e in range(NE):
@@ -183,28 +204,29 @@
 
     loop(0, I // 2, d_step, 4)
 
-    wait_recv(rbuf.at[pl.ds(0, (NE * (NA - 1)) // NA)], 1)
-    for e in range(NE):
-        rt[pl.ds(e * L2, L2), :] = rbuf[e].astype(F32).T.astype(BF16)
-
-    def g_step(k):
-        base = k * 8
-        lhs = jnp.concatenate(
-            [dbuf[pl.ds(base, 8), :, e].reshape(8 * C, L2) for e in range(NE)], axis=1
-        )
-        gtf[pl.ds(pl.multiple_of(base * C, 8 * C), 8 * C), :] = dot(lhs, rt[...], NN)
-
-    loop(0, I // 8, g_step, 3)
-    for q in range(NC):
+    def rows_of(ah, q):
+        x = lbuf[ah * NZ + q].astype(F32).T
         for h in range(2):
-            gsend[q, pl.ds(h * I, I), :] = gtf[pl.ds(2 * q + h, I, stride=C), :].astype(BF16)
+            ltf[ah, pl.ds(2 * q + h, I, stride=CH), :] = x[h * JP:h * JP + I]
+
+    for k in arrival:
+        q = (z + NZ - k) & (NZ - 1)
+        block = lbuf.at[yh * NZ + q]
+        got = lbuf.at[0, pl.ds(0, S - SB if k == 0 else S)]
+        pltpu.make_async_copy(got, got, nsem.at[k]).wait()
+        if k in relayed:
+            copy(block, block, ssem.at[2], fsem.at[k], (r, (1 - yh) * NZ + z, s))
+        rows_of(yh, q)
+        if k == relayed[0]:
+            wait_recv(rbuf.at[pl.ds(0, (NE * (NA // 2 - 1)) // NA)], 1)
+            for t in range(NS // 2):
+                part = rbuf.at[:, pl.ds(pl.multiple_of((2 * t + core) * SB, SB), SB)]
+                send(part, part, 9, sibling)
+
+    wait_recv(rbuf.at[pl.ds(0, NE // 2)], 9)
 
     def half_step(ah):
         lh = ltf.at[ah]
-        for q in range(NZ):
-            x = lbuf[ah * NZ + q].astype(F32).T
-            for h in range(2):
-                lh[pl.ds(2 * q + h, I, stride=CH), :] = x[h * JP:h * JP + I]
 
         def o_step(k):
             base = k * IB
@@ -235,13 +257,31 @@
 
         loop(0, NE, send_piece)
 
-    wait_recv(gtf.at[pl.ds(0, (NZ * NS - 1) * SB // 2)], 0)
     half_step(yh)
-    wait_recv(lbuf.at[pl.ds(0, NZ)], 2)
-    loop(1, NC, lambda k: send(gsend.at[(c + k) & (NC - 1)], grecv.at[c], 3, col_peer(k)))
+
+    for k in direct + relayed[::-1]:
+        pltpu.make_async_copy(lbuf.at[0], lbuf.at[0], fsem.at[k]).wait()
+        rows_of(1 - yh, (z + NZ - k) & (NZ - 1))
     half_step(1 - yh)
     wrecv[ip] = wsend[ip]
-    grecv[c] = gsend[c]
+
+    for e in range(NE):
+        rt[pl.ds(e * L2, L2), :] = rbuf[e].astype(F32).T.astype(BF16)
+
+    def g_step(k):
+        base = k * 8
+        lhs = jnp.concatenate(
+            [dbuf[pl.ds(base, 8), :, e].reshape(8 * C, L2) for e in range(NE)], axis=1
+        )
+        gtf[pl.ds(pl.multiple_of(base * C, 8 * C), 8 * C), :] = dot(lhs, rt[...], NN)
+
+    loop(0, I // 8, g_step, 3)
+    for q in range(NC):
+        for h in range(2):
+            gsend[q, pl.ds(h * I, I), :] = gtf[pl.ds(2 * q + h, I, stride=C), :].astype(BF16)
+
+    partner = (r, (1 - yh) * NZ + z, s)
+    send(gsend.at[pl.ds(pl.multiple_of((1 - yh) * NZ, NZ), NZ)], gx, 10, partner)
 
     for ah in range(2):
         for q in range((I * CH) // S):
@@ -261,6 +301,9 @@
 
     loop(0, NE // 2, h_step, 2)
 
+    for t in range(NS // 2):
+        send(hsend.at[:, pl.ds(pl.multiple_of((2 * t + 1 - core) * SB, SB), SB)], hx.at[t], 11, sibling)
+
     wait_recv(wrecv.at[pl.ds(0, NP - 1)], 4)
     total = wrecv[0].astype(F32)
     for q in range(1, NP):
@@ -269,14 +312,20 @@
     loop(1, NZ, lambda k: send(w1send, zrecv.at[z], 6, z_peer(k)))
     zrecv[z] = w1send[...]
 
-    def h_piece(t):
-        return hsend.at[
-            pl.ds(pl.multiple_of((t >> log2(NS)) * NER, NER), NER),
-            pl.ds(pl.multiple_of((t & (NS - 1)) * SB, SB), SB),
-        ]
-
-    loop(1, NA, lambda k: send(h_piece((ia + k) & (NA - 1)), hrecv.at[ia], 5, row_seq_peer(k)))
-    hrecv[ia] = hsend[pl.ds(erow, NER), pl.ds(srow, SB), :]
+    wait_recv(hx, 11)
+    for t in range(NS // 2):
+        h1send[t] = (
+            hsend[:, pl.ds(pl.multiple_of((2 * t + core) * SB, SB), SB), :].astype(F32) + hx[t].astype(F32)
+        ).astype(BF16)
+    own = r * (NS // 2) + (s >> 1)
+    for k in range(1, NR):
+        for t in range(NS // 2):
+            q = (r + k) & (NR - 1)
+            send(h1send.at[t, pl.ds(pl.multiple_of(q * NER, NER), NER)], hrecv.at[own], 5, (q, c, 2 * t + core))
+    for k in range(1, NS // 2):
+        t = ((s >> 1) + k) & (NS // 2 - 1)
+        send(h1send.at[t, pl.ds(erow, NER)], hrecv.at[own], 5, (r, c, 2 * t + core))
+    hrecv[own] = h1send[s >> 1, pl.ds(erow, NER)]
 
     def p_step(k):
         rhs = jnp.concatenate(
@@ -302,33 +351,43 @@
     loop(1, NP, lambda k: send(w2send, wall.at[ip], 7, plane_peer(k)))
     wall[ip] = w2send[...]
 
-    wait_recv(grecv.at[pl.ds(0, NC - 1)], 3)
-    total = grecv[0].astype(F32)
-    for q in range(1, NC):
-        total = total + grecv[q].astype(F32)
+    wait_recv(gx, 10)
     pad = jnp.zeros((JP - I, S), F32)
-    t = jnp.concatenate([total[:I], pad, total[I:], pad], axis=0) * (1.0 / S)
-    g2send[...] = t.T.astype(BF16)
-    loop(1, NS, lambda k: send(
-        g2send.at[pl.ds(pl.multiple_of(((s + k) & (NS - 1)) * SB, SB), SB)], g2recv.at[s], 8, seq_peer(k)))
-    g2recv[s] = g2send[pl.ds(srow, SB), :]
+    for q in range(NZ):
+        t = (gsend[yh * NZ + q].astype(F32) + gx[q].astype(F32)) * (1.0 / S)
+        g1send[q] = jnp.concatenate([t[:I], pad, t[I:], pad], axis=0).T.astype(BF16)
+    for k in range(1, NS):
+        t = (s + k) & (NS - 1)
+        send(g1send.at[z, pl.ds(pl.multiple_of(t * SB, SB), SB)], grecv.at[z * NS + s], 3, (r, c, t))
+
+    def g_send(k):
+        q = (z + k) & (NZ - 1)
+        for t in range(NS):
+            send(g1send.at[q, pl.ds(t * SB, SB)], grecv.at[z * NS + s], 3, (r, yh * NZ + q, t))
+
+    loop(1, NZ, g_send)
+    grecv[z * NS + s] = g1send[z, pl.ds(srow, SB), :]
 
     loop(I // 4, I // 2, p_step, 4)
 
-    wait_recv(hrecv.at[pl.ds(0, NA - 1)], 5)
+    wait_recv(hrecv.at[pl.ds(0, NA // 2 - 1)], 5)
     for e in range(NER):
         total = hrecv[0, e].astype(F32)
-        for q in range(1, NA):
+        for q in range(1, NA // 2):
             total = total + hrecv[q, e].astype(F32)
         total = total * (1.0 / S)
         for h in range(2):
             rg[:, 2 * e + h, :] = total[:, h * JP:h * JP + J]
 
-    wait_recv(g2recv.at[pl.ds(0, NS - 1)], 8)
+    wait_recv(grecv.at[pl.ds(0, NZ * NS - 1)], 3)
+    parts = []
+    for q in range(NS):
+        total = grecv[q].astype(F32)
+        for t in range(1, NZ):
+            total = total + grecv[t * NS + q].astype(F32)
+        parts.append(total)
     for h in range(2):
-        lg[:, h, :] = jnp.concatenate(
-            [g2recv[q].astype(F32)[:, h * JP:h * JP + I] for q in range(NS)], axis=1
-        )
+        lg[:, h, :] = jnp.concatenate([x[:, h * JP:h * JP + I] for x in parts], axis=1)
 
     wait_recv(wall.at[pl.ds(0, NP - 1)], 7)
     for ah in range(2):
@@ -338,14 +397,16 @@
                 wg[pl.ds(ah * CH * 2 * NE + 2 * e + h, CH, stride=2 * NE), :] = x[:, h * CP:(h + 1) * CP]
 
     wait_send(gtf.at[pl.ds(0, (NZ * NS - 1) * SB // 2)], 0)
-    wait_send(rbuf.at[pl.ds(0, (NE * (NA - 1)) // NA)], 1)
+    wait_send(rbuf.at[pl.ds(0, (NE * (NA // 2 - 1)) // NA)], 1)
+    wait_send(rbuf.at[pl.ds(0, NE // 2)], 9)
     wait_send(lbuf.at[pl.ds(0, NZ)], 2)
-    wait_send(grecv.at[pl.ds(0, NC - 1)], 3)
+    wait_send(grecv.at[pl.ds(0, NZ * NS - 1)], 3)
+    wait_send(gx, 10)
+    wait_send(hx, 11)
     wait_send(wrecv.at[pl.ds(0, NP - 1)], 4)
-    wait_send(hrecv.at[pl.ds(0, NA - 1)], 5)
+    wait_send(hrecv.at[pl.ds(0, NA // 2 - 1)], 5)
     wait_send(zrecv.at[pl.ds(0, NZ - 1)], 6)
     wait_send(wall.at[pl.ds(0, NP - 1)], 7)
-    wait_send(g2recv.at[pl.ds(0, NS - 1)], 8)
 
 
 def finish(*refs):
@@ -375,6 +436,7 @@
     vmem = pl.BlockSpec(memory_space=pltpu.VMEM)
     hbm = pl.BlockSpec(memory_space=pl.ANY)
     scratch = [
+        pltpu.VMEM((1, CP), F32),
         pltpu.VMEM(left.shape, BF16),
         pltpu.VMEM(right.shape, BF16),
         pltpu.VMEM((SB * 2 * NER, 128), F32),
@@ -395,11 +457,13 @@
         pltpu.VMEM((I, L2, 2 * CP), BF16),
         pltpu.VMEM((I * C, S), F32),
         pltpu.VMEM((NC, 2 * I, S), BF16),
-        pltpu.VMEM((NC, 2 * I, S), BF16),
+        pltpu.VMEM((NZ, 2 * I, S), BF16),
+        pltpu.VMEM((NZ, S, L2), BF16),
+        pltpu.VMEM((NZ * NS, SB, L2), BF16),
         pltpu.VMEM((NE, S, L2), BF16),
-        pltpu.VMEM((NA, NER, SB, L2), BF16),
-        pltpu.VMEM((S, L2), BF16),
-        pltpu.VMEM((NS, SB, L2), BF16),
+        pltpu.VMEM((NS // 2, NE, SB, L2), BF16),
+        pltpu.VMEM((NS // 2, NE, SB, L2), BF16),
+        pltpu.VMEM((NA // 2, NER, SB, L2), BF16),
         pltpu.VMEM((NP, CH, 2 * CP), BF16),
         pltpu.VMEM((NP, CH, 2 * CP), BF16),
         pltpu.VMEM((CH, 2 * CP), BF16),
@@ -407,15 +471,17 @@
         pltpu.VMEM((CH, 2 * CP), BF16),
         pltpu.VMEM((NP, CH, 2 * CP), BF16),
         pltpu.VMEM((NE * CH, 2 * CP), F32),
-        pltpu.SemaphoreType.DMA((9,)),
-        pltpu.SemaphoreType.DMA((9,)),
-        pltpu.SemaphoreType.DMA((4,)),
+        pltpu.SemaphoreType.DMA((12,)),
+        pltpu.SemaphoreType.DMA((12,)),
+        pltpu.SemaphoreType.DMA((NZ,)),
+        pltpu.SemaphoreType.DMA((NZ,)),
+        pltpu.SemaphoreType.DMA((5,)),
     ]
     shapes = ((I, J, CP), BF16), (left.shape, F32), (right.shape, F32), (projection.shape, F32)
     results = pl.pallas_call(
         functools.partial(kernel, n),
         out_shape=tuple(pltpu.VMEM(shape, dtype) for shape, dtype in shapes),
-        in_specs=[hbm] * 4 + [vmem],
+        in_specs=[hbm] * 5,
         out_specs=(vmem,) * 4,
         scratch_shapes=scratch,
         compiler_params=pltpu.CompilerParams(

time: 52.9 us -> 48.8 us (0.922)
  Pallas kernels: 52.2 us -> 48.1 us
    pallas_call x1, Pallas kernels: 51.1 us -> 47 us  [body(): pl.pallas_call(functools.partial(kernel, n), out_shape=tuple((pltpu.VMEM(...]
where the time goes in v4:
time: 48.8 us; the launch traced here: 48.7 us
  Pallas kernels  48.1 us (99%)
  between operations  0.64 us (1%)
    pallas_call x1, Pallas kernels, body(): pl.pallas_call(functools.partial(kernel, n), out_shape=tuple((pltpu.VMEM(...  47 us
    pallas_call x1, Pallas kernels, body(): pl.pallas_call(finish, out_shape=tuple((jax.ShapeDtypeStruct(shape, dtype...  1.09 us

profile of v4, /device:TPU:1, one launch (start us, length us, event | category | flops | bytes accessed | tf_op | source)
XLA Modules:
  0.0 48.7 jit_solution(7565342109927516875)
XLA Ops:
  0.6 47.0 %shard_map.84 = (bf16[48,48,128]{2,1,0:T(8,128)(2,1)S(1)}, f32[32,2,192]{2,1,0:T(2,128)S(1)}, f32[32,8,48]{2,1,0:T(8,128)S(1)}, f32[1024,128]{1,0:T(8,128)S(1)}) custom-call(bf16[32,2,192]{2,1,0:T(2,128)(2,1)} %left.1, bf16[32,8,48]{2,1,0:T(8,128)(2,1)} %right.1, bf16[48,48,128]{2,1,0:T(8,128)(2,1)} %cot_in.1, bf16[1024,128]{1,0:T(8,128)(2,1)} %w_in.1, ...), custom_call_target="tpu_custom_call" | custom-call | tf_op jit(solution)/shard_map/pallas_call | solution.py:481
  47.6 1.1 %shard_map.85 = (bf16[48,48,128]{2,1,0:T(8,128)(2,1)}, f32[32,2,192]{2,1,0:T(2,128)}, f32[32,8,48]{2,1,0:T(8,128)}, f32[1024,128]{1,0:T(8,128)}) custom-call(bf16[48,48,128]{2,1,0:T(8,128)(2,1)S(1)} %get-tuple-element.8.refs_0_, f32[32,2,192]{2,1,0:T(2,128)S(1)} %get-tuple-element.9.refs_1_, f32[32,8,48]{2,1,0:T(8,128)S(1)} %get-tuple-element.10.refs_2_, ...), custom_call_target="tpu_custom_call" | custom-call | tf_op jit(solution)/shard_map/pallas_call | solution.py:491

commit v5 on v4

--- a/solution.py
+++ b/solution.py
@@ -101,6 +101,7 @@
     near = sorted(range(NZ), key=lambda k: min(k, NZ - k))
     relayed = [k for k in near if min(k, NZ - k) > NZ // 4]
     direct = [k for k in near if k not in relayed]
+    NG = NZ + len(direct)
 
     def greet_z(k):
         t = (z + k) & (NZ - 1)
@@ -276,12 +277,37 @@
         gtf[pl.ds(pl.multiple_of(base * C, 8 * C), 8 * C), :] = dot(lhs, rt[...], NN)
 
     loop(0, I // 8, g_step, 3)
-    for q in range(NC):
-        for h in range(2):
-            gsend[q, pl.ds(h * I, I), :] = gtf[pl.ds(2 * q + h, I, stride=C), :].astype(BF16)
-
-    partner = (r, (1 - yh) * NZ + z, s)
-    send(gsend.at[pl.ds(pl.multiple_of((1 - yh) * NZ, NZ), NZ)], gx, 10, partner)
+
+    def g_rows(half, k):
+        q = half * NZ + ((z + k) & (NZ - 1))
+        return [gtf[pl.ds(2 * q + h, I, stride=C), :] for h in range(2)]
+
+    for j, k in enumerate(relayed):
+        gsend[j] = jnp.concatenate(g_rows(1 - yh, k), axis=0).astype(BF16)
+    send(gsend, gx, 10, (r, (1 - yh) * NZ + z, s))
+
+    pad = jnp.zeros((JP - I, S), F32)
+
+    def g_block(rows):
+        return (jnp.concatenate([rows[0], pad, rows[1], pad], axis=0) * (1.0 / S)).T.astype(BF16)
+
+    for j, k in enumerate(direct):
+        g1send[k] = g_block(g_rows(yh, k))
+        g1send[NZ + j] = g_block(g_rows(1 - yh, k))
+
+    def g_to(half, k, slot):
+        q = (z + k) & (NZ - 1)
+        for t in range(NS):
+            send(g1send.at[slot, pl.ds(t * SB, SB)], grecv.at[slot * NS + s], 3, (r, half * NZ + q, t))
+
+    for k in range(1, NS):
+        t = (s + k) & (NS - 1)
+        send(g1send.at[0, pl.ds(pl.multiple_of(t * SB, SB), SB)], grecv.at[s], 3, (r, c, t))
+    grecv[s] = g1send[0, pl.ds(srow, SB), :]
+    for j, k in enumerate(direct):
+        if k > 0:
+            g_to(yh, k, k)
+        g_to(1 - yh, k, NZ + j)
 
     for ah in range(2):
         for q in range((I * CH) // S):
@@ -311,7 +337,6 @@
     w1send[...] = total.astype(BF16)
     loop(1, NZ, lambda k: send(w1send, zrecv.at[z], 6, z_peer(k)))
     zrecv[z] = w1send[...]
-
     wait_recv(hx, 11)
     for t in range(NS // 2):
         h1send[t] = (
@@ -343,6 +368,12 @@
 
     loop(0, I // 4, p_step, 4)
 
+    wait_recv(gx, 10)
+    for j, k in enumerate(relayed):
+        rows = g_rows(yh, k)
+        g1send[k] = g_block([rows[h] + gx[j, pl.ds(h * I, I), :].astype(F32) for h in range(2)])
+        g_to(yh, k, k)
+
     wait_recv(zrecv.at[pl.ds(0, NZ - 1)], 6)
     total = zrecv[0].astype(F32)
     for q in range(1, NZ):
@@ -350,23 +381,6 @@
     w2send[...] = (total * (1.0 / S)).astype(BF16)
     loop(1, NP, lambda k: send(w2send, wall.at[ip], 7, plane_peer(k)))
     wall[ip] = w2send[...]
-
-    wait_recv(gx, 10)
-    pad = jnp.zeros((JP - I, S), F32)
-    for q in range(NZ):
-        t = (gsend[yh * NZ + q].astype(F32) + gx[q].astype(F32)) * (1.0 / S)
-        g1send[q] = jnp.concatenate([t[:I], pad, t[I:], pad], axis=0).T.astype(BF16)
-    for k in range(1, NS):
-        t = (s + k) & (NS - 1)
-        send(g1send.at[z, pl.ds(pl.multiple_of(t * SB, SB), SB)], grecv.at[z * NS + s], 3, (r, c, t))
-
-    def g_send(k):
-        q = (z + k) & (NZ - 1)
-        for t in range(NS):
-            send(g1send.at[q, pl.ds(t * SB, SB)], grecv.at[z * NS + s], 3, (r, yh * NZ + q, t))
-
-    loop(1, NZ, g_send)
-    grecv[z * NS + s] = g1send[z, pl.ds(srow, SB), :]
 
     loop(I // 4, I // 2, p_step, 4)
 
@@ -379,16 +393,6 @@
         for h in range(2):
             rg[:, 2 * e + h, :] = total[:, h * JP:h * JP + J]
 
-    wait_recv(grecv.at[pl.ds(0, NZ * NS - 1)], 3)
-    parts = []
-    for q in range(NS):
-        total = grecv[q].astype(F32)
-        for t in range(1, NZ):
-            total = total + grecv[t * NS + q].astype(F32)
-        parts.append(total)
-    for h in range(2):
-        lg[:, h, :] = jnp.concatenate([x[:, h * JP:h * JP + I] for x in parts], axis=1)
-
     wait_recv(wall.at[pl.ds(0, NP - 1)], 7)
     for ah in range(2):
         for e in range(NE):
@@ -396,11 +400,21 @@
             for h in range(2):
                 wg[pl.ds(ah * CH * 2 * NE + 2 * e + h, CH, stride=2 * NE), :] = x[:, h * CP:(h + 1) * CP]
 
+    wait_recv(grecv.at[pl.ds(0, NG * NS - 1)], 3)
+    parts = []
+    for q in range(NS):
+        total = grecv[q].astype(F32)
+        for t in range(1, NG):
+            total = total + grecv[t * NS + q].astype(F32)
+        parts.append(total)
+    for h in range(2):
+        lg[:, h, :] = jnp.concatenate([x[:, h * JP:h * JP + I] for x in parts], axis=1)
+
     wait_send(gtf.at[pl.ds(0, (NZ * NS - 1) * SB // 2)], 0)
     wait_send(rbuf.at[pl.ds(0, (NE * (NA // 2 - 1)) // NA)], 1)
     wait_send(rbuf.at[pl.ds(0, NE // 2)], 9)
     wait_send(lbuf.at[pl.ds(0, NZ)], 2)
-    wait_send(grecv.at[pl.ds(0, NZ * NS - 1)], 3)
+    wait_send(grecv.at[pl.ds(0, NG * NS - 1)], 3)
     wait_send(gx, 10)
     wait_send(hx, 11)
     wait_send(wrecv.at[pl.ds(0, NP - 1)], 4)
@@ -432,6 +446,8 @@
     L2 = 2 * JP
     NER = right.shape[1] // 2
     NE = NER * NR
+
+    far = sum(min(k, NZ - k) > NZ // 4 for k in range(NZ))
 
     vmem = pl.BlockSpec(memory_space=pltpu.VMEM)
     hbm = pl.BlockSpec(memory_space=pl.ANY)
@@ -456,10 +472,10 @@
         pltpu.VMEM((I, 2, NE, CH, L2), BF16),
         pltpu.VMEM((I, L2, 2 * CP), BF16),
         pltpu.VMEM((I * C, S), F32),
-        pltpu.VMEM((NC, 2 * I, S), BF16),
-        pltpu.VMEM((NZ, 2 * I, S), BF16),
-        pltpu.VMEM((NZ, S, L2), BF16),
-        pltpu.VMEM((NZ * NS, SB, L2), BF16),
+        pltpu.VMEM((far, 2 * I, S), BF16),
+        pltpu.VMEM((far, 2 * I, S), BF16),
+        pltpu.VMEM((2 * NZ - far, S, L2), BF16),
+        pltpu.VMEM(((2 * NZ - far) * NS, SB, L2), BF16),
         pltpu.VMEM((NE, S, L2), BF16),
         pltpu.VMEM((NS // 2, NE, SB, L2), BF16),
         pltpu.VMEM((NS // 2, NE, SB, L2), BF16),

time: 48.8 us -> 46.7 us (0.957)
  Pallas kernels: 48.1 us -> 46 us
    pallas_call x1, Pallas kernels: 47 us -> 44.9 us  [body(): pl.pallas_call(functools.partial(kernel, n), out_shape=tuple((pltpu.VMEM(...]
where the time goes in v5:
time: 46.7 us; the launch traced here: 46.6 us
  Pallas kernels  46 us (99%)
  between operations  0.64 us (1%)
    pallas_call x1, Pallas kernels, body(): pl.pallas_call(functools.partial(kernel, n), out_shape=tuple((pltpu.VMEM(...  44.9 us
    pallas_call x1, Pallas kernels, body(): pl.pallas_call(finish, out_shape=tuple((jax.ShapeDtypeStruct(shape, dtype...  1.09 us

profile of v5, /device:TPU:1, one launch (start us, length us, event | category | flops | bytes accessed | tf_op | source)
XLA Modules:
  0.0 46.6 jit_solution(17465407042683848938)
XLA Ops:
  0.6 44.9 %shard_map.84 = (bf16[48,48,128]{2,1,0:T(8,128)(2,1)S(1)}, f32[32,2,192]{2,1,0:T(2,128)S(1)}, f32[32,8,48]{2,1,0:T(8,128)S(1)}, f32[1024,128]{1,0:T(8,128)S(1)}) custom-call(bf16[32,2,192]{2,1,0:T(2,128)(2,1)} %left.1, bf16[32,8,48]{2,1,0:T(8,128)(2,1)} %right.1, bf16[48,48,128]{2,1,0:T(8,128)(2,1)} %cot_in.1, bf16[1024,128]{1,0:T(8,128)(2,1)} %w_in.1, ...), custom_call_target="tpu_custom_call" | custom-call | tf_op jit(solution)/shard_map/pallas_call | solution.py:497
  45.6 1.1 %shard_map.85 = (bf16[48,48,128]{2,1,0:T(8,128)(2,1)}, f32[32,2,192]{2,1,0:T(2,128)}, f32[32,8,48]{2,1,0:T(8,128)}, f32[1024,128]{1,0:T(8,128)}) custom-call(bf16[48,48,128]{2,1,0:T(8,128)(2,1)S(1)} %get-tuple-element.8.refs_0_, f32[32,2,192]{2,1,0:T(2,128)S(1)} %get-tuple-element.9.refs_1_, f32[32,8,48]{2,1,0:T(8,128)S(1)} %get-tuple-element.10.refs_2_, ...), custom_call_target="tpu_custom_call" | custom-call | tf_op jit(solution)/shard_map/pallas_call | solution.py:507

commit v6 on v5

--- a/solution.py
+++ b/solution.py
@@ -304,10 +304,8 @@
         t = (s + k) & (NS - 1)
         send(g1send.at[0, pl.ds(pl.multiple_of(t * SB, SB), SB)], grecv.at[s], 3, (r, c, t))
     grecv[s] = g1send[0, pl.ds(srow, SB), :]
-    for j, k in enumerate(direct):
-        if k > 0:
-            g_to(yh, k, k)
-        g_to(1 - yh, k, NZ + j)
+    for k in direct[1:]:
+        g_to(yh, k, k)
 
     for ah in range(2):
         for q in range((I * CH) // S):
@@ -351,6 +349,9 @@
         t = ((s >> 1) + k) & (NS // 2 - 1)
         send(h1send.at[t, pl.ds(erow, NER)], hrecv.at[own], 5, (r, c, 2 * t + core))
     hrecv[own] = h1send[s >> 1, pl.ds(erow, NER)]
+
+    for j, k in enumerate(direct):
+        g_to(1 - yh, k, NZ + j)
 
     def p_step(k):
         rhs = jnp.concatenate(

time: 46.7 us -> 46.9 us (level)
  no operation moved by 1% of the time
where the time goes in v6:
time: 46.9 us; the launch traced here: 46.8 us
  Pallas kernels  46.2 us (99%)
  between operations  0.64 us (1%)
    pallas_call x1, Pallas kernels, body(): pl.pallas_call(functools.partial(kernel, n), out_shape=tuple((pltpu.VMEM(...  45.1 us
    pallas_call x1, Pallas kernels, body(): pl.pallas_call(finish, out_shape=tuple((jax.ShapeDtypeStruct(shape, dtype...  1.09 us

profile of v6, /device:TPU:1, one launch (start us, length us, event | category | flops | bytes accessed | tf_op | source)
XLA Modules:
  0.0 46.8 jit_solution(9435180348289900049)
XLA Ops:
  0.6 45.1 %shard_map.84 = (bf16[48,48,128]{2,1,0:T(8,128)(2,1)S(1)}, f32[32,2,192]{2,1,0:T(2,128)S(1)}, f32[32,8,48]{2,1,0:T(8,128)S(1)}, f32[1024,128]{1,0:T(8,128)S(1)}) custom-call(bf16[32,2,192]{2,1,0:T(2,128)(2,1)} %left.1, bf16[32,8,48]{2,1,0:T(8,128)(2,1)} %right.1, bf16[48,48,128]{2,1,0:T(8,128)(2,1)} %cot_in.1, bf16[1024,128]{1,0:T(8,128)(2,1)} %w_in.1, ...), custom_call_target="tpu_custom_call" | custom-call | tf_op jit(solution)/shard_map/pallas_call | solution.py:498
  45.7 1.1 %shard_map.85 = (bf16[48,48,128]{2,1,0:T(8,128)(2,1)}, f32[32,2,192]{2,1,0:T(2,128)}, f32[32,8,48]{2,1,0:T(8,128)}, f32[1024,128]{1,0:T(8,128)}) custom-call(bf16[48,48,128]{2,1,0:T(8,128)(2,1)S(1)} %get-tuple-element.8.refs_0_, f32[32,2,192]{2,1,0:T(2,128)S(1)} %get-tuple-element.9.refs_1_, f32[32,8,48]{2,1,0:T(8,128)S(1)} %get-tuple-element.10.refs_2_, ...), custom_call_target="tpu_custom_call" | custom-call | tf_op jit(solution)/shard_map/pallas_call | solution.py:508

commit v7 on v6

--- a/solution.py
+++ b/solution.py
@@ -465,14 +465,14 @@
         pltpu.VMEM((NS, SB, L2), BF16),
         pltpu.VMEM((NER, SB, L2), BF16),
         pltpu.VMEM((NC, S, L2), BF16),
-        pltpu.VMEM((2, I * CH, S), F32),
+        pltpu.VMEM((2, I * CH + CH, S), F32),
         pltpu.VMEM((S, I * C), BF16),
         pltpu.VMEM((NE, S, L2), BF16),
         pltpu.VMEM((NE * L2, S), BF16),
         pltpu.VMEM((I, 2, NE, CH, L2), BF16),
         pltpu.VMEM((I, 2, NE, CH, L2), BF16),
         pltpu.VMEM((I, L2, 2 * CP), BF16),
-        pltpu.VMEM((I * C, S), F32),
+        pltpu.VMEM((I * C + C, S), F32),
         pltpu.VMEM((far, 2 * I, S), BF16),
         pltpu.VMEM((far, 2 * I, S), BF16),
         pltpu.VMEM((2 * NZ - far, S, L2), BF16),

time: 46.9 us -> 46.9 us (level)
  no operation moved by 1% of the time
where the time goes in v7:
time: 46.9 us; the launch traced here: 46.8 us
  Pallas kernels  46.2 us (99%)
  between operations  0.64 us (1%)
    pallas_call x1, Pallas kernels, body(): pl.pallas_call(functools.partial(kernel, n), out_shape=tuple((pltpu.VMEM(...  45.1 us
    pallas_call x1, Pallas kernels, body(): pl.pallas_call(finish, out_shape=tuple((jax.ShapeDtypeStruct(shape, dtype...  1.09 us

profile of v7, /device:TPU:1, one launch (start us, length us, event | category | flops | bytes accessed | tf_op | source)
XLA Modules:
  0.0 46.8 jit_solution(14658788216169984795)
XLA Ops:
  0.6 45.1 %shard_map.84 = (bf16[48,48,128]{2,1,0:T(8,128)(2,1)S(1)}, f32[32,2,192]{2,1,0:T(2,128)S(1)}, f32[32,8,48]{2,1,0:T(8,128)S(1)}, f32[1024,128]{1,0:T(8,128)S(1)}) custom-call(bf16[32,2,192]{2,1,0:T(2,128)(2,1)} %left.1, bf16[32,8,48]{2,1,0:T(8,128)(2,1)} %right.1, bf16[48,48,128]{2,1,0:T(8,128)(2,1)} %cot_in.1, bf16[1024,128]{1,0:T(8,128)(2,1)} %w_in.1, ...), custom_call_target="tpu_custom_call" | custom-call | tf_op jit(solution)/shard_map/pallas_call | solution.py:498
  45.7 1.1 %shard_map.85 = (bf16[48,48,128]{2,1,0:T(8,128)(2,1)}, f32[32,2,192]{2,1,0:T(2,128)}, f32[32,8,48]{2,1,0:T(8,128)}, f32[1024,128]{1,0:T(8,128)}) custom-call(bf16[48,48,128]{2,1,0:T(8,128)(2,1)S(1)} %get-tuple-element.8.refs_0_, f32[32,2,192]{2,1,0:T(2,128)S(1)} %get-tuple-element.9.refs_1_, f32[32,8,48]{2,1,0:T(8,128)S(1)} %get-tuple-element.10.refs_2_, ...), custom_call_target="tpu_custom_call" | custom-call | tf_op jit(solution)/shard_map/pallas_call | solution.py:508
